TPU v7x, 128 devices: a whole 4x4x4 slice. The times are simulated.
128 devices in a mesh: seq: 4 (over z_hi, core), tp: 32 (over x, y, z_lo).
Axes of the slice: x: 4, y: 4, z: 4 (z_hi: 2, z_lo: 2; z = z_hi * 2 + z_lo), core: 2. Of those that a mesh axis runs over, the one named last changes fastest.
Arguments:
- tokens: bfloat16 [2048, 8192], P('seq', 'tp'), may hold values from -6 to 6
- up_weight: bfloat16 [128, 6, 256, 256], P(('seq', 'tp')), may hold values from -0.15625 to 0.15625
- down_weight: bfloat16 [128, 6, 256, 256], P(('seq', 'tp')), may hold values from -0.078125 to 0.078125
- block_mask: int32 [128, 6], P(('seq', 'tp')), may hold values from 0 to 1, as said below
- cotangent: bfloat16 [2048, 8192], P('seq', 'tp'), may hold values from -1.5 to 1.5
Outputs:
- output: bfloat16 [2048, 8192], P('seq', 'tp')
- grad_tokens: bfloat16 [2048, 8192], P('seq', 'tp')
- grad_up: float32 [128, 6, 256, 256], P(('seq', 'tp'))
- grad_down: float32 [128, 6, 256, 256], P(('seq', 'tp'))
Inputs may be any that keep to these rules, and one draw needn't show every extreme that they name: `block_mask`: entries are 0 or 1; level 0 is 1 for every hidden group; for every owner index and level, at least one of the 4 hidden groups with that owner index has a 1.
All inputs are finite; a program needn't handle non-finite values.
Results may differ from a plain program's by a relative error of at most 0.0056.
Values may be sent and summed in bfloat16 or wider, within the bound.
A program may use at most 128 MiB of HBM per device.

v0:
```python
import functools
import math

import jax
import jax.numpy as jnp
from jax import lax
from jax.experimental import pallas as pl
from jax.experimental.pallas import tpu as pltpu
from jax.sharding import PartitionSpec as P

MESH = pl.DeviceIdType.MESH
F32 = jnp.float32
BF16 = jnp.bfloat16
ROWS = 512
PART = 128
PIECES = ROWS // PART
FIRST = PIECES // 2
TILE = 256
PER_TILE = TILE // PART
THIRDS = 3
G = 256
LEVELS = 6
WIDE = LEVELS * G
NEAR = {"x": 4, "y": 2}
FAR = {"x": 5, "y": 3}
SCALE = math.sqrt(2.0 / math.pi)
CUBE = 0.044715


def numbering():
    keys = []
    for which in range(2):
        keys += [(name, which, j) for name in ("z1", "z3", "zr", "out1", "out3", "half") for j in range(PIECES)]
        keys += [
            (name, axis, which, slot, j)
            for name in ("near", "far", "term", "sum")
            for axis in "xy"
            for slot in range(2)
            for j in range(PIECES)
        ]
        keys += [("weight", which)] + [("grad", which, k) for k in range(LEVELS // THIRDS)]
    keys += [("last", axis, j) for axis in "xy" for j in range(PIECES)]
    return {key: n for n, key in enumerate(keys)}


def family(key):
    name = key[0]
    if name in ("weight", "grad"):
        return key
    if name in ("near", "far", "term", "sum"):
        return name, key[2], key[3]
    if name == "last":
        return (name,)
    return {"z1": "z", "z3": "z", "zr": "middle", "half": "middle", "out1": "out", "out3": "out"}[name], key[1]


NUMBER = numbering()
COPIES = len(NUMBER)
FAMILIES = {name: n for n, name in enumerate(dict.fromkeys(family(key) for key in NUMBER))}

ORDER = (
    ("ox", 0, 2), ("oz", 0, 2), ("ox", 0, 3), ("sd",), ("oz", 0, 0), ("oz", 0, 1), ("ox", 1, 2), ("su",),
    ("ox", 0, 0), ("oz", 0, 3), ("oz", 1, 0), ("rx", 0, 0, 2), ("ox", 0, 1), ("rx", 0, 0, 3), ("rz", 0, 1),
    ("rx", 1, 0, 2), ("ox", 1, 3), ("rz", 0, 2), ("rz", 0, 0), ("rz", 0, 3), ("ox", 1, 0), ("oz", 1, 3),
    ("rx", 0, 0, 0), ("F", 0, 1), ("rz", 1, 0), ("ox", 1, 1), ("oz", 1, 1), ("rx", 0, 0, 1), ("rx", 1, 0, 3),
    ("ot", 0, 1), ("tw",), ("ot", 0, 2), ("ot", 0, 0), ("oz", 1, 2), ("rx", 1, 0, 0), ("F", 0, 0), ("rx", 0, 1, 1),
    ("rz", 1, 3), ("TN", 0, 0, 1), ("ot", 1, 0), ("rx", 1, 0, 1), ("ot", 0, 3), ("th", 0), ("J", 0, 0, 2),
    ("rz", 1, 1), ("rx", 0, 1, 0), ("rz", 1, 2), ("B", 0, 1), ("Z", 0, 0, 3), ("rx", 0, 1, 2), ("ta", 0, 0),
    ("ot", 1, 3), ("TF", 0, 0, 0), ("TN", 0, 0, 0), ("Z", 0, 0, 2), ("rx", 0, 1, 3), ("TN", 1, 0, 1),
    ("rx", 1, 1, 0), ("ot", 1, 1), ("ot", 1, 2), ("F", 1, 0), ("TF", 0, 1, 0), ("rx", 1, 1, 3), ("W", ("weight", 1)),
    ("TF", 1, 0, 1), ("S", 0, 1, 1), ("S", 0, 0, 0), ("J", 0, 0, 3), ("W", ("weight", 0)), ("F", 1, 1), ("ta", 0, 1),
    ("W", ("z", 0)), ("S", 0, 0, 1), ("S", 0, 1, 0), ("TN", 0, 1, 0), ("W", ("near", 0, 0)), ("TF", 0, 0, 1),
    ("rx", 1, 1, 2), ("Z", 1, 0, 2), ("TF", 0, 1, 1), ("rx", 1, 1, 1), ("ta", 1, 1), ("TN", 0, 1, 1), ("B", 0, 0),
    ("TF", 1, 0, 0), ("J", 0, 1, 1), ("ta", 1, 0), ("J", 0, 1, 0), ("S", 0, 1, 3), ("W", ("near", 1, 0)),
    ("S", 0, 0, 3), ("C", 0, 0, 2), ("W", ("far", 0, 0)), ("Z", 0, 1, 0), ("S", 0, 1, 2), ("B", 1, 1),
    ("TF", 1, 1, 1), ("Z", 1, 0, 3), ("J", 0, 0, 0), ("W", ("z", 1)), ("TN", 1, 1, 1), ("J", 0, 0, 1),
    ("S", 1, 1, 3), ("B", 1, 0), ("TF", 1, 1, 0), ("S", 1, 1, 0), ("S", 1, 1, 1), ("W", ("far", 1, 0)),
    ("S", 1, 1, 2), ("W", ("near", 0, 1)), ("J", 0, 1, 3), ("C", 0, 1, 0), ("TN", 1, 1, 0), ("Z", 1, 1, 0),
    ("G", 1, 1), ("Z", 1, 1, 1), ("J", 1, 1, 3), ("C", 0, 1, 1), ("th", 1), ("J", 1, 1, 0), ("TN", 1, 0, 0),
    ("S", 1, 0, 3), ("PO", 0, 0), ("S", 1, 0, 0), ("W", ("far", 0, 1)), ("S", 1, 0, 2), ("J", 1, 1, 1),
    ("C", 0, 1, 3), ("Z", 0, 1, 1), ("W", ("near", 1, 1)), ("J", 0, 1, 2), ("G", 0, 0), ("J", 1, 1, 2),
    ("C", 1, 1, 3), ("S", 0, 0, 2), ("PO", 0, 1), ("RL", 3), ("C", 1, 1, 0), ("S", 1, 0, 1), ("G", 1, 0),
    ("C", 1, 1, 1), ("J", 1, 0, 0), ("C", 0, 1, 2), ("PO", 1, 3), ("RL", 0), ("PO", 0, 3), ("J", 1, 0, 3),
    ("W", ("far", 1, 1)), ("C", 1, 1, 2), ("PO", 1, 0), ("RL", 1), ("G", 0, 1), ("J", 1, 0, 2), ("PO", 0, 2),
    ("RL", 2), ("GS", 1, 0), ("PO", 1, 1), ("J", 1, 0, 1), ("PO", 1, 2), ("C", 0, 0, 1), ("W", ("term", 0, 1)),
    ("C", 1, 0, 3), ("GS", 0, 0), ("GS", 1, 1), ("FIN", 0, 1), ("FIN", 1, 3), ("C", 1, 0, 0), ("W", ("sum", 0, 0)),
    ("C", 0, 0, 3), ("FIN", 0, 3), ("C", 0, 0, 0), ("FIN", 0, 0), ("FIN", 0, 2), ("GS", 0, 1), ("W", ("term", 1, 1)),
    ("FIN", 1, 0), ("C", 1, 0, 2), ("FIN", 1, 2), ("C", 1, 0, 1), ("FIN", 1, 1),
    ("W", ("middle", 0), ("middle", 1), ("out", 0), ("term", 0, 0), ("out", 1), ("sum", 0, 1), ("grad", 1, 1), ("sum", 1, 1), ("term", 1, 0), ("grad", 0, 0), ("last",), ("grad", 1, 0), ("sum", 1, 0), ("grad", 0, 1)),
)


def flip(index, bit):
    return index + bit - 2 * bit * lax.rem(lax.div(index, bit), 2)


def kernel(
    tok, cot, up, down, mask, out, gtok, gup, gdown,
    held, held_t, raw, uall, dall, uall_t, dall_t, act, act_t, gpre, slope,
    term_send, term_recv, near_term, sum_send, sum_recv, base, z_term,
    half_send, half_recv, last_recv, z_send, z_recv,
    grad_own, grad_peer, grad_recv,
    sends, recvs, local,
):
    shared = (tok, cot)
    seq, tp = lax.axis_index("seq"), lax.axis_index("tp")
    place = {
        "core": (flip(seq, 1), tp),
        "z1": (seq, flip(tp, 1)),
        "z3": (flip(seq, 2), flip(tp, 1)),
        "x1": (seq, flip(tp, 8)),
        "x3": (seq, flip(flip(tp, 8), 16)),
        "y1": (seq, flip(tp, 2)),
        "y3": (seq, flip(flip(tp, 2), 4)),
    }

    def remote(src, dst, key, target):
        return pltpu.make_async_remote_copy(
            src_ref=src,
            dst_ref=dst,
            send_sem=sends.at[FAMILIES[family(key)]],
            recv_sem=recvs.at[NUMBER[key]],
            device_id=place[target],
            device_id_type=MESH,
        )

    def rows(slot, j):
        start = slot * ROWS + j * PART
        return pl.ds(start if isinstance(j, int) else pl.multiple_of(start, PART), PART)

    def piece(j):
        return pl.ds(j * PART, PART)

    def columns(level):
        return pl.ds(level * G, G)

    def transfer(key):
        name, rest = key[0], key[1:]
        if name == "weight":
            if rest[0] == 0:
                return remote(uall.at[:, pl.ds(0, G)], uall.at[:, pl.ds(G, G)], key, "core")
            return remote(dall.at[pl.ds(0, G)], dall.at[pl.ds(G, G)], key, "core")
        if name == "grad":
            at = pl.ds(rest[1] * THIRDS, THIRDS)
            return remote(grad_peer.at[rest[0], at], grad_recv.at[rest[0], at], key, "core")
        if name == "last":
            a, j = "xy".index(rest[0]), rest[1]
            return remote(term_recv.at[0, a, rows(0, j)], last_recv.at[a, piece(j)], key, rest[0] + "3")
        if name in ("near", "far", "term", "sum"):
            axis, which, slot, j = rest
            a, at = "xy".index(axis), rows(slot, j)
            if name == "near":
                src = held.at[which, 0, at] if slot else shared[which].at[piece(j)]
                return remote(src, held.at[which, NEAR[axis], at], key, axis + "1")
            if name == "far":
                return remote(held.at[which, NEAR[axis], at], held.at[which, FAR[axis], at], key, axis + "3")
            if name == "term":
                target = axis + ("1" if (which, slot) == (0, 0) else "3")
                return remote(term_send.at[which, a, at], term_recv.at[which, a, at], key, target)
            return remote(sum_send.at[which, a, at], sum_recv.at[which, a, at], key, axis + "1")
        which, j = rest
        if name == "z1":
            return remote(shared[which].at[piece(j)], held.at[which, 1, rows(0, j)], key, "z1")
        if name == "z3":
            return remote(shared[which].at[piece(j)], held.at[which, 1, rows(1, j)], key, "z3")
        onward = "z3" if j < FIRST else "z1"
        if name == "zr":
            return remote(held.at[which, 1, rows(int(j >= FIRST), j)], held.at[which, 0, rows(1, j)], key, onward)
        if name == "half":
            return remote(half_send.at[which, piece(j)], half_recv.at[which, piece(j)], key, onward)
        slot = int(name == "out3")
        return remote(z_send.at[which, rows(slot, j)], z_recv.at[which, rows(slot, j)], key, "z3" if slot else "z1")

    started, landed, copied, sent = set(), set(), set(), set()

    def send(*keys):
        for key in keys:
            started.add(key)
            transfer(key).start()

    def need(*keys):
        for key in keys:
            if key not in landed:
                landed.add(key)
                transfer(key).wait_recv()

    own = [
        pltpu.make_async_copy(shared[which], held.at[which, 0, pl.ds(0, ROWS)], local.at[which])
        for which in range(2)
    ]
    loads = [pltpu.make_async_copy(ref, raw.at[which], local.at[2 + which]) for which, ref in enumerate((up, down))]
    for copy in loads + own:
        copy.start()

    barrier = pltpu.get_barrier_semaphore()
    for target in place.values():
        pl.semaphore_signal(barrier, inc=1, device_id=target, device_id_type=MESH)
    pl.semaphore_wait(barrier, len(place))

    def scale_up(k, carry):
        factor = mask[0, k].astype(F32)
        uall[pl.ds(pl.multiple_of(k * G, G), G), pl.ds(0, G)] = (raw[0, k].astype(F32) * factor).astype(BF16)
        return carry

    def scale_down(k, carry):
        factor = mask[0, k].astype(F32)
        dall[pl.ds(0, G), pl.ds(pl.multiple_of(k * G, G), G)] = (raw[1, k].astype(F32) * factor).astype(BF16)
        return carry

    def wide(which, at):
        return jnp.concatenate([held[which, level, at] for level in range(LEVELS)], axis=1)

    def tile(slot, t):
        return pl.ds(slot * ROWS + t * TILE, TILE)

    def own_z(which, j):
        send(("z1", which, j), ("z3", which, j))

    def own_xy(which, j):
        send(("near", "x", which, 0, j), ("near", "y", which, 0, j))

    def relay_z(which, j):
        need(("z1" if j < FIRST else "z3", which, j))
        send(("zr", which, j))

    def other(which, j):
        need(("zr", which, j))
        send(("near", "x", which, 1, j), ("near", "y", which, 1, j))

    def relay_xy(which, slot, j):
        for axis in "xy":
            need(("near", axis, which, slot, j))
            send(("far", axis, which, slot, j))

    def mask_up():
        loads[0].wait()
        lax.fori_loop(0, LEVELS, scale_up, 0)
        send(("weight", 0))

    def mask_down():
        loads[1].wait()
        lax.fori_loop(0, LEVELS, scale_down, 0)
        send(("weight", 1))

    def turn_weights():
        need(("weight", 0), ("weight", 1))

        def body(k, carry):
            at = pl.ds(pl.multiple_of(k * G, G), G)
            dall_t[at, :] = dall[:, at].T
            uall_t[:, at] = uall[at, :].T
            return carry

        lax.fori_loop(0, LEVELS, body, 0)

    def turn_held(slot):
        def body(k, carry):
            at = pl.ds(pl.multiple_of(k * G, G), G)
            held_t[at, pl.ds(slot * ROWS, ROWS)] = held[0, k, pl.ds(slot * ROWS, ROWS)].T
            return carry

        lax.fori_loop(0, LEVELS, body, 0)

    def turn_act(slot, t):
        act_t[:, tile(slot, t)] = act[tile(slot, t), :].T

    def inputs(which, slot, t):
        if slot == 0 and ("own", which) not in copied:
            copied.add(("own", which))
            own[which].wait()
        for j in range(t * PER_TILE, (t + 1) * PER_TILE):
            need(("z3" if slot else "z1", which, j))
            for axis in "xy":
                need(("far", axis, which, slot, j))

    def forward(slot, t):
        inputs(0, slot, t)
        need(("weight", 0), ("weight", 1))
        at = tile(slot, t)
        pre = jnp.dot(wide(0, at), uall[...], preferred_element_type=F32)
        square = pre * pre
        tanh = jnp.tanh(SCALE * pre * (1.0 + CUBE * square))
        cdf = 0.5 + 0.5 * tanh
        act[at, :] = (pre * cdf).astype(BF16)
        slope[at, :] = cdf + (0.5 * SCALE) * pre * (1.0 - tanh * tanh) * (1.0 + (3.0 * CUBE) * square)

    def backward(slot, t):
        inputs(1, slot, t)
        at = tile(slot, t)
        gact = jnp.dot(wide(1, at), dall_t[...], preferred_element_type=F32)
        gpre[at, :] = (gact * slope[at, :]).astype(BF16)

    def product(which, slot, t, level):
        if which:
            return jnp.dot(gpre[tile(slot, t), :], uall_t[:, columns(level)], preferred_element_type=F32)
        return jnp.dot(act[tile(slot, t), :], dall[:, columns(level)], preferred_element_type=F32)

    def far_terms(which, slot, t):
        for a, axis in enumerate("xy"):
            term_send[which, a, tile(slot, t)] = product(which, slot, t, FAR[axis]).astype(BF16)

    def near_terms(which, slot, t):
        at = tile(slot, t)
        for a, axis in enumerate("xy"):
            near_term[which, a, at] = product(which, slot, t, NEAR[axis])
        z_term[which, at] = product(which, slot, t, 1)
        base[which, at] = product(which, slot, t, 0)

    def send_term(which, slot, j):
        send(("term", "x", which, slot, j), ("term", "y", which, slot, j))

    def hand_on(j):
        for axis in "xy":
            need(("term", axis, 0, 0, j))
            send(("last", axis, j))

    def join(which, slot, j):
        at = rows(slot, j)
        for a, axis in enumerate("xy"):
            total = near_term[which, a, at]
            if (which, slot) != (0, 0):
                need(("term", axis, which, slot, j))
                total = total + term_recv[which, a, at].astype(F32)
            sum_send[which, a, at] = total.astype(BF16)
            send(("sum", axis, which, slot, j))

    def collect(which, slot, j):
        at = rows(slot, j)
        need(("sum", "x", which, slot, j), ("sum", "y", which, slot, j))
        total = base[which, at] + sum_recv[which, 0, at].astype(F32) + sum_recv[which, 1, at].astype(F32)
        if slot == 0:
            base[which, at] = total
        else:
            half_send[which, piece(j)] = total.astype(BF16)
            send(("half", which, j))

    def plain(which, slot, j):
        z_send[which, rows(slot, j)] = z_term[which, rows(slot, j)].astype(BF16)
        send(("out3" if slot else "out1", which, j))

    def pass_on(which, j):
        slot = int(j >= FIRST)
        at = rows(slot, j)
        need(("half", which, j))
        z_send[which, at] = (z_term[which, at] + half_recv[which, piece(j)].astype(F32)).astype(BF16)
        send(("out3" if slot else "out1", which, j))

    def finish(which, j):
        need(("out1", which, j), ("out3", which, j))
        total = base[which, rows(0, j)] + z_recv[which, rows(0, j)].astype(F32) + z_recv[which, rows(1, j)].astype(F32)
        if which == 0:
            need(("last", "x", j), ("last", "y", j))
            total = total + last_recv[0, piece(j)].astype(F32) + last_recv[1, piece(j)].astype(F32)
        (gtok if which else out)[piece(j), :] = total.astype(BF16)

    def grads(which, third):
        def body(k, carry):
            at = pl.ds(pl.multiple_of(k * G, G), G)
            if which:
                both = jnp.dot(act_t[...], held[1, k], preferred_element_type=F32)
                grad_own[1, k] = both[:G]
                grad_peer[1, k] = both[G:]
            else:
                both = jnp.dot(held_t[at, :], gpre[...], preferred_element_type=F32)
                grad_own[0, k] = both[:, :G]
                grad_peer[0, k] = both[:, G:]
            return carry

        lax.fori_loop(third * THIRDS, (third + 1) * THIRDS, body, 0)
        send(("grad", which, third))

    def write_grad(which, k):
        return pltpu.make_async_copy(grad_own.at[which, k], (gdown if which else gup).at[k], local.at[4 + which * LEVELS + k])

    def grads_sum(which, third):
        need(("grad", which, third))

        def body(k, carry):
            grad_own[which, k] = (grad_own[which, k] + grad_recv[which, k]) * mask[0, k].astype(F32)
            write_grad(which, k).start()
            return carry

        lax.fori_loop(third * THIRDS, (third + 1) * THIRDS, body, 0)

    def finish_sends(*names):
        for name in names:
            sent.add(name)
            if name[0] in ("weight", "grad"):
                transfer(name).wait_send()
            else:
                pltpu.make_async_remote_copy(
                    src_ref=held.at[0, 0],
                    dst_ref=held.at[0, 0],
                    send_sem=sends.at[FAMILIES[name]],
                    recv_sem=recvs.at[0],
                    device_id=place["z1"],
                    device_id_type=MESH,
                ).wait_send()

    steps = {
        "W": finish_sends,
        "oz": own_z, "ox": own_xy, "rz": relay_z, "ot": other, "rx": relay_xy, "su": mask_up, "sd": mask_down,
        "tw": turn_weights, "th": turn_held, "ta": turn_act, "F": forward, "B": backward, "TF": far_terms,
        "TN": near_terms, "S": send_term, "RL": hand_on, "J": join, "C": collect, "Z": plain, "PO": pass_on,
        "FIN": finish, "G": grads, "GS": grads_sum,
    }
    for step in ORDER:
        steps[step[0]](*step[1:])

    assert started == landed == set(NUMBER)
    for which in range(2):
        for k in range(LEVELS):
            write_grad(which, k).wait()
    assert sent == set(FAMILIES)


def hand_out(*refs):
    sources, results, sems = refs[:4], refs[4:8], refs[8]
    copies = []
    for src, dst in zip(sources, results):
        if len(src.shape) == 2:
            pairs = [(src, dst)]
        else:
            pairs = [(src.at[pl.ds(k, 2)], dst.at[pl.ds(k, 2)]) for k in range(0, LEVELS, 2)]
        for a, b in pairs:
            copies.append(pltpu.make_async_copy(a, b, sems.at[len(copies)]))
    for copy in copies:
        copy.start()
    for copy in copies:
        copy.wait()


def shards(tokens, up_weight, down_weight, block_mask, cotangent):
    anywhere = pl.BlockSpec(memory_space=pl.ANY)
    vmem = pl.BlockSpec(memory_space=pltpu.VMEM)
    both = 2 * ROWS
    result = (
        jax.ShapeDtypeStruct((ROWS, G), BF16),
        jax.ShapeDtypeStruct((ROWS, G), BF16),
        jax.ShapeDtypeStruct((LEVELS, G, G), F32),
        jax.ShapeDtypeStruct((LEVELS, G, G), F32),
    )
    operands = [pltpu.with_memory_space_constraint(a, pltpu.HBM) for a in (tokens, cotangent, up_weight[0], down_weight[0])]
    worked = pl.pallas_call(
        kernel,
        out_shape=tuple(pltpu.VMEM(a.shape, a.dtype) for a in result),
        in_specs=[anywhere, anywhere, anywhere, anywhere, pl.BlockSpec(memory_space=pltpu.SMEM)],
        out_specs=(vmem, vmem, anywhere, anywhere),
        scratch_shapes=[
            pltpu.VMEM((2, LEVELS, both, G), BF16),
            pltpu.VMEM((WIDE, both), BF16),
            pltpu.VMEM((2, LEVELS, G, G), BF16),
            pltpu.VMEM((WIDE, 2 * G), BF16),
            pltpu.VMEM((2 * G, WIDE), BF16),
            pltpu.VMEM((2 * G, WIDE), BF16),
            pltpu.VMEM((WIDE, 2 * G), BF16),
            pltpu.VMEM((both, 2 * G), BF16),
            pltpu.VMEM((2 * G, both), BF16),
            pltpu.VMEM((both, 2 * G), BF16),
            pltpu.VMEM((both, 2 * G), F32),
            pltpu.VMEM((2, 2, both, G), BF16),
            pltpu.VMEM((2, 2, both, G), BF16),
            pltpu.VMEM((2, 2, both, G), F32),
            pltpu.VMEM((2, 2, both, G), BF16),
            pltpu.VMEM((2, 2, both, G), BF16),
            pltpu.VMEM((2, both, G), F32),
            pltpu.VMEM((2, both, G), F32),
            pltpu.VMEM((2, ROWS, G), BF16),
            pltpu.VMEM((2, ROWS, G), BF16),
            pltpu.VMEM((2, ROWS, G), BF16),
            pltpu.VMEM((2, both, G), BF16),
            pltpu.VMEM((2, both, G), BF16),
            pltpu.VMEM((2, LEVELS, G, G), F32),
            pltpu.VMEM((2, LEVELS, G, G), F32),
            pltpu.VMEM((2, LEVELS, G, G), F32),
            pltpu.SemaphoreType.DMA((len(FAMILIES),)),
            pltpu.SemaphoreType.DMA((COPIES,)),
            pltpu.SemaphoreType.DMA((4 + 2 * LEVELS,)),
        ],
        compiler_params=pltpu.CompilerParams(
            collective_id=0, has_side_effects=True, vmem_limit_bytes=58 * 1024 * 1024
        ),
    )(*operands, block_mask)
    worked = [pltpu.with_memory_space_constraint(a, pltpu.VMEM) for a in worked]
    output, grad_tokens, grad_up, grad_down = pl.pallas_call(
        hand_out,
        out_shape=result,
        in_specs=[anywhere] * 4,
        out_specs=(anywhere,) * 4,
        scratch_shapes=[pltpu.SemaphoreType.DMA((8,))],
        compiler_params=pltpu.CompilerParams(vmem_limit_bytes=1024 * 1024),
    )(*worked)
    return output, grad_tokens, grad_up[None], grad_down[None]


def solution(mesh):
    placed = (
        P("seq", "tp"),
        P(("seq", "tp"), None, None, None),
        P(("seq", "tp"), None, None, None),
        P(("seq", "tp"), None),
        P("seq", "tp"),
    )
    return jax.shard_map(
        shards,
        mesh=mesh,
        in_specs=placed,
        out_specs=(
            P("seq", "tp"),
            P("seq", "tp"),
            P(("seq", "tp"), None, None, None),
            P(("seq", "tp"), None, None, None),
        ),
        check_vma=False,
    )
```

profile of v0, /device:TPU:0, one launch (start us, length us, event | category | flops | bytes accessed | tf_op | source)
XLA Modules:
  0.0 67.1 jit_solution(14268278071990057181)
XLA Ops:
  0.6 64.6 %shard_map.84 = (bf16[512,256]{1,0:T(8,128)(2,1)S(1)}, bf16[512,256]{1,0:T(8,128)(2,1)S(1)}, f32[6,256,256]{2,1,0:T(8,128)S(1)}, f32[6,256,256]{2,1,0:T(8,128)S(1)}) custom-call(bf16[512,256]{1,0:T(8,128)(2,1)} %tok.1, bf16[512,256]{1,0:T(8,128)(2,1)} %cot.1, bf16[6,256,256]{2,1,0:T(8,128)(2,1)} %bitcast.4, bf16[6,256,256]{2,1,0:T(8,128)(2,1)} %bitcast.5, ...), custom_call_target="tpu_custom_call" | custom-call | tf_op jit(solution)/shard_map/pallas_call | solution.py:444
  65.2 1.9 %shard_map.85 = (bf16[512,256]{1,0:T(8,128)(2,1)}, bf16[512,256]{1,0:T(8,128)(2,1)}, f32[6,256,256]{2,1,0:T(8,128)}, f32[6,256,256]{2,1,0:T(8,128)}) custom-call(bf16[512,256]{1,0:T(8,128)(2,1)S(1)} %get-tuple-element.12.refs_0_, bf16[512,256]{1,0:T(8,128)(2,1)S(1)} %get-tuple-element.13.refs_1_, f32[6,256,256]{2,1,0:T(8,128)S(1)} %get-tuple-element.14.refs_2_, ...), custom_call_target="tpu_custom_call" | custom-call | tf_op jit(solution)/shard_map/pallas_call | solution.py:485
where the time goes:
time: 67.2 us; the launch traced here: 67.1 us
  Pallas kernels  66.5 us (99%)
    pallas_call x1, Pallas kernels, shards(): pl.pallas_call(kernel, out_shape=tuple((pltpu.VMEM(a.shape, a.dtype) for...  64.6 us
    pallas_call x1, Pallas kernels, shards(): pl.pallas_call(hand_out, out_shape=result, in_specs=[anywhere] * 4, out_s...  1.9 us

commit v1 on v0

--- a/solution.py
+++ b/solution.py
@@ -59,34 +59,33 @@
 FAMILIES = {name: n for n, name in enumerate(dict.fromkeys(family(key) for key in NUMBER))}
 
 ORDER = (
-    ("ox", 0, 2), ("oz", 0, 2), ("ox", 0, 3), ("sd",), ("oz", 0, 0), ("oz", 0, 1), ("ox", 1, 2), ("su",),
-    ("ox", 0, 0), ("oz", 0, 3), ("oz", 1, 0), ("rx", 0, 0, 2), ("ox", 0, 1), ("rx", 0, 0, 3), ("rz", 0, 1),
-    ("rx", 1, 0, 2), ("ox", 1, 3), ("rz", 0, 2), ("rz", 0, 0), ("rz", 0, 3), ("ox", 1, 0), ("oz", 1, 3),
-    ("rx", 0, 0, 0), ("F", 0, 1), ("rz", 1, 0), ("ox", 1, 1), ("oz", 1, 1), ("rx", 0, 0, 1), ("rx", 1, 0, 3),
-    ("ot", 0, 1), ("tw",), ("ot", 0, 2), ("ot", 0, 0), ("oz", 1, 2), ("rx", 1, 0, 0), ("F", 0, 0), ("rx", 0, 1, 1),
-    ("rz", 1, 3), ("TN", 0, 0, 1), ("ot", 1, 0), ("rx", 1, 0, 1), ("ot", 0, 3), ("th", 0), ("J", 0, 0, 2),
-    ("rz", 1, 1), ("rx", 0, 1, 0), ("rz", 1, 2), ("B", 0, 1), ("Z", 0, 0, 3), ("rx", 0, 1, 2), ("ta", 0, 0),
-    ("ot", 1, 3), ("TF", 0, 0, 0), ("TN", 0, 0, 0), ("Z", 0, 0, 2), ("rx", 0, 1, 3), ("TN", 1, 0, 1),
-    ("rx", 1, 1, 0), ("ot", 1, 1), ("ot", 1, 2), ("F", 1, 0), ("TF", 0, 1, 0), ("rx", 1, 1, 3), ("W", ("weight", 1)),
-    ("TF", 1, 0, 1), ("S", 0, 1, 1), ("S", 0, 0, 0), ("J", 0, 0, 3), ("W", ("weight", 0)), ("F", 1, 1), ("ta", 0, 1),
-    ("W", ("z", 0)), ("S", 0, 0, 1), ("S", 0, 1, 0), ("TN", 0, 1, 0), ("W", ("near", 0, 0)), ("TF", 0, 0, 1),
-    ("rx", 1, 1, 2), ("Z", 1, 0, 2), ("TF", 0, 1, 1), ("rx", 1, 1, 1), ("ta", 1, 1), ("TN", 0, 1, 1), ("B", 0, 0),
-    ("TF", 1, 0, 0), ("J", 0, 1, 1), ("ta", 1, 0), ("J", 0, 1, 0), ("S", 0, 1, 3), ("W", ("near", 1, 0)),
-    ("S", 0, 0, 3), ("C", 0, 0, 2), ("W", ("far", 0, 0)), ("Z", 0, 1, 0), ("S", 0, 1, 2), ("B", 1, 1),
-    ("TF", 1, 1, 1), ("Z", 1, 0, 3), ("J", 0, 0, 0), ("W", ("z", 1)), ("TN", 1, 1, 1), ("J", 0, 0, 1),
-    ("S", 1, 1, 3), ("B", 1, 0), ("TF", 1, 1, 0), ("S", 1, 1, 0), ("S", 1, 1, 1), ("W", ("far", 1, 0)),
-    ("S", 1, 1, 2), ("W", ("near", 0, 1)), ("J", 0, 1, 3), ("C", 0, 1, 0), ("TN", 1, 1, 0), ("Z", 1, 1, 0),
-    ("G", 1, 1), ("Z", 1, 1, 1), ("J", 1, 1, 3), ("C", 0, 1, 1), ("th", 1), ("J", 1, 1, 0), ("TN", 1, 0, 0),
-    ("S", 1, 0, 3), ("PO", 0, 0), ("S", 1, 0, 0), ("W", ("far", 0, 1)), ("S", 1, 0, 2), ("J", 1, 1, 1),
-    ("C", 0, 1, 3), ("Z", 0, 1, 1), ("W", ("near", 1, 1)), ("J", 0, 1, 2), ("G", 0, 0), ("J", 1, 1, 2),
-    ("C", 1, 1, 3), ("S", 0, 0, 2), ("PO", 0, 1), ("RL", 3), ("C", 1, 1, 0), ("S", 1, 0, 1), ("G", 1, 0),
-    ("C", 1, 1, 1), ("J", 1, 0, 0), ("C", 0, 1, 2), ("PO", 1, 3), ("RL", 0), ("PO", 0, 3), ("J", 1, 0, 3),
-    ("W", ("far", 1, 1)), ("C", 1, 1, 2), ("PO", 1, 0), ("RL", 1), ("G", 0, 1), ("J", 1, 0, 2), ("PO", 0, 2),
-    ("RL", 2), ("GS", 1, 0), ("PO", 1, 1), ("J", 1, 0, 1), ("PO", 1, 2), ("C", 0, 0, 1), ("W", ("term", 0, 1)),
-    ("C", 1, 0, 3), ("GS", 0, 0), ("GS", 1, 1), ("FIN", 0, 1), ("FIN", 1, 3), ("C", 1, 0, 0), ("W", ("sum", 0, 0)),
-    ("C", 0, 0, 3), ("FIN", 0, 3), ("C", 0, 0, 0), ("FIN", 0, 0), ("FIN", 0, 2), ("GS", 0, 1), ("W", ("term", 1, 1)),
-    ("FIN", 1, 0), ("C", 1, 0, 2), ("FIN", 1, 2), ("C", 1, 0, 1), ("FIN", 1, 1),
-    ("W", ("middle", 0), ("middle", 1), ("out", 0), ("term", 0, 0), ("out", 1), ("sum", 0, 1), ("grad", 1, 1), ("sum", 1, 1), ("term", 1, 0), ("grad", 0, 0), ("last",), ("grad", 1, 0), ("sum", 1, 0), ("grad", 0, 1)),
+    ("oz", 0, 1), ("ox", 1, 3), ("ox", 0, 1), ("oz", 0, 3), ("sd",), ("su",), ("ox", 0, 2), ("ox", 0, 0),
+    ("oz", 0, 2), ("oz", 0, 0), ("rx", 0, 0, 1), ("ox", 0, 3), ("oz", 1, 2), ("rx", 1, 0, 3), ("ox", 1, 0),
+    ("rz", 0, 0), ("ox", 1, 1), ("rz", 0, 3), ("rx", 0, 0, 0), ("rz", 0, 1), ("rz", 1, 2), ("ox", 1, 2),
+    ("rx", 0, 0, 2), ("oz", 1, 1), ("oz", 1, 3), ("rx", 0, 0, 3), ("ot", 0, 0), ("rx", 1, 0, 0), ("F", 0, 0),
+    ("oz", 1, 0), ("rz", 0, 2), ("ot", 0, 3), ("rx", 1, 0, 2), ("ot", 1, 2), ("ta", 0, 0), ("ot", 0, 1),
+    ("rz", 1, 1), ("rx", 0, 1, 0), ("rx", 1, 0, 1), ("TN", 0, 0, 0), ("tw",), ("rz", 1, 0), ("rz", 1, 3),
+    ("rx", 0, 1, 3), ("ot", 1, 1), ("F", 0, 1), ("ot", 0, 2), ("rx", 0, 1, 1), ("TF", 0, 0, 1), ("TF", 0, 0, 0),
+    ("TN", 0, 0, 1), ("Z", 0, 0, 2), ("rx", 1, 1, 2), ("ot", 1, 0), ("J", 0, 0, 0), ("Z", 0, 0, 3), ("ot", 1, 3),
+    ("B", 0, 0), ("rx", 1, 1, 1), ("rx", 0, 1, 2), ("J", 0, 0, 3), ("F", 1, 0), ("TF", 0, 1, 0), ("S", 0, 1, 1),
+    ("S", 0, 0, 1), ("J", 0, 0, 2), ("ta", 0, 1), ("S", 0, 1, 0), ("TN", 0, 1, 0), ("B", 0, 1), ("TN", 1, 0, 1),
+    ("rx", 1, 1, 0), ("S", 0, 0, 2), ("S", 0, 0, 3), ("ta", 1, 0), ("F", 1, 1), ("TF", 0, 1, 1), ("S", 0, 1, 3),
+    ("th", 0), ("ta", 1, 1), ("J", 0, 1, 0), ("rx", 1, 1, 3), ("J", 0, 1, 1), ("TF", 1, 0, 1), ("W", ("weight", 1)),
+    ("TN", 0, 1, 1), ("W", ("weight", 0)), ("B", 1, 0), ("S", 0, 1, 2), ("TF", 1, 1, 0), ("S", 1, 1, 0),
+    ("W", ("z", 0)), ("TN", 1, 0, 0), ("Z", 0, 1, 0), ("W", ("near", 0, 0)), ("th", 1), ("B", 1, 1), ("J", 0, 1, 3),
+    ("TF", 1, 0, 0), ("S", 1, 1, 1), ("Z", 1, 0, 2), ("Z", 1, 0, 3), ("TN", 1, 1, 0), ("Z", 0, 1, 1), ("J", 0, 0, 1),
+    ("W", ("near", 1, 0)), ("TF", 1, 1, 1), ("S", 1, 1, 2), ("S", 1, 1, 3), ("J", 0, 1, 2), ("W", ("far", 0, 0)),
+    ("C", 0, 1, 1), ("J", 1, 1, 0), ("G", 0, 1), ("C", 0, 1, 0), ("W", ("z", 1)), ("C", 0, 1, 3), ("S", 1, 0, 2),
+    ("TN", 1, 1, 1), ("J", 1, 1, 1), ("Z", 1, 1, 1), ("G", 1, 0), ("Z", 1, 1, 0), ("S", 1, 0, 0), ("PO", 0, 1),
+    ("W", ("far", 1, 0)), ("J", 1, 1, 2), ("J", 1, 1, 3), ("C", 0, 1, 2), ("S", 1, 0, 3), ("PO", 0, 0),
+    ("S", 1, 0, 1), ("C", 0, 0, 1), ("PO", 0, 3), ("W", ("near", 0, 1)), ("GS", 0, 1), ("G", 1, 1), ("J", 1, 0, 2),
+    ("C", 1, 1, 1), ("C", 0, 0, 3), ("RL", 1), ("GS", 1, 0), ("S", 0, 0, 0), ("C", 1, 1, 2), ("RL", 3),
+    ("W", ("near", 1, 1)), ("C", 1, 1, 0), ("RL", 2), ("PO", 0, 2), ("W", ("far", 0, 1)), ("C", 1, 1, 3),
+    ("J", 1, 0, 3), ("G", 0, 0), ("PO", 1, 1), ("J", 1, 0, 0), ("PO", 1, 2), ("RL", 0), ("C", 1, 0, 2),
+    ("C", 0, 0, 2), ("PO", 1, 0), ("J", 1, 0, 1), ("PO", 1, 3), ("GS", 1, 1), ("C", 1, 0, 3), ("FIN", 0, 2),
+    ("FIN", 0, 1), ("FIN", 1, 2), ("C", 0, 0, 0), ("FIN", 0, 3), ("FIN", 0, 0), ("GS", 0, 0), ("C", 1, 0, 0),
+    ("W", ("far", 1, 1)), ("FIN", 1, 0), ("C", 1, 0, 1), ("FIN", 1, 1), ("FIN", 1, 3),
+    ("W", ("middle", 0), ("middle", 1), ("out", 0), ("sum", 0, 0), ("term", 0, 1), ("term", 0, 0), ("sum", 0, 1), ("term", 1, 1), ("out", 1), ("sum", 1, 1), ("grad", 0, 1), ("term", 1, 0), ("grad", 1, 0), ("grad", 1, 1), ("sum", 1, 0), ("last",), ("grad", 0, 0)),
 )
 
 

time: 67.2 us -> 67.5 us (level)
  no operation moved by 1% of the time
where the time goes in v1:
time: 67.5 us; the launch traced here: 67.3 us
  Pallas kernels  66.7 us (99%)
    pallas_call x1, Pallas kernels, shards(): pl.pallas_call(kernel, out_shape=tuple((pltpu.VMEM(a.shape, a.dtype) for...  64.8 us
    pallas_call x1, Pallas kernels, shards(): pl.pallas_call(hand_out, out_shape=result, in_specs=[anywhere] * 4, out_s...  1.9 us

profile of v1, /device:TPU:0, one launch (start us, length us, event | category | flops | bytes accessed | tf_op | source)
XLA Modules:
  0.0 67.3 jit_solution(8750757360691213958)
XLA Ops:
  0.6 64.8 %shard_map.84 = (bf16[512,256]{1,0:T(8,128)(2,1)S(1)}, bf16[512,256]{1,0:T(8,128)(2,1)S(1)}, f32[6,256,256]{2,1,0:T(8,128)S(1)}, f32[6,256,256]{2,1,0:T(8,128)S(1)}) custom-call(bf16[512,256]{1,0:T(8,128)(2,1)} %tok.1, bf16[512,256]{1,0:T(8,128)(2,1)} %cot.1, bf16[6,256,256]{2,1,0:T(8,128)(2,1)} %bitcast.4, bf16[6,256,256]{2,1,0:T(8,128)(2,1)} %bitcast.5, ...), custom_call_target="tpu_custom_call" | custom-call | tf_op jit(solution)/shard_map/pallas_call | solution.py:443
  65.4 1.9 %shard_map.85 = (bf16[512,256]{1,0:T(8,128)(2,1)}, bf16[512,256]{1,0:T(8,128)(2,1)}, f32[6,256,256]{2,1,0:T(8,128)}, f32[6,256,256]{2,1,0:T(8,128)}) custom-call(bf16[512,256]{1,0:T(8,128)(2,1)S(1)} %get-tuple-element.12.refs_0_, bf16[512,256]{1,0:T(8,128)(2,1)S(1)} %get-tuple-element.13.refs_1_, f32[6,256,256]{2,1,0:T(8,128)S(1)} %get-tuple-element.14.refs_2_, ...), custom_call_target="tpu_custom_call" | custom-call | tf_op jit(solution)/shard_map/pallas_call | solution.py:484

commit v2 on v1

--- a/solution.py
+++ b/solution.py
@@ -39,8 +39,12 @@
             for j in range(PIECES)
         ]
         keys += [("weight", which)] + [("grad", which, k) for k in range(LEVELS // THIRDS)]
-    keys += [("last", axis, j) for axis in "xy" for j in range(PIECES)]
+    keys += [("last", axis, j) for axis in "xy" for j in PASSED]
     return {key: n for n, key in enumerate(keys)}
+
+
+def passed(which, slot, j):
+    return which == 0 and slot == 0 and j in PASSED
 
 
 def family(key):
@@ -50,42 +54,44 @@
     if name in ("near", "far", "term", "sum"):
         return name, key[2], key[3]
     if name == "last":
-        return (name,)
+        return name, key[2]
     return {"z1": "z", "z3": "z", "zr": "middle", "half": "middle", "out1": "out", "out3": "out"}[name], key[1]
 
 
+PASSED = (2, 3)
 NUMBER = numbering()
 COPIES = len(NUMBER)
 FAMILIES = {name: n for n, name in enumerate(dict.fromkeys(family(key) for key in NUMBER))}
 
 ORDER = (
-    ("oz", 0, 1), ("ox", 1, 3), ("ox", 0, 1), ("oz", 0, 3), ("sd",), ("su",), ("ox", 0, 2), ("ox", 0, 0),
-    ("oz", 0, 2), ("oz", 0, 0), ("rx", 0, 0, 1), ("ox", 0, 3), ("oz", 1, 2), ("rx", 1, 0, 3), ("ox", 1, 0),
-    ("rz", 0, 0), ("ox", 1, 1), ("rz", 0, 3), ("rx", 0, 0, 0), ("rz", 0, 1), ("rz", 1, 2), ("ox", 1, 2),
-    ("rx", 0, 0, 2), ("oz", 1, 1), ("oz", 1, 3), ("rx", 0, 0, 3), ("ot", 0, 0), ("rx", 1, 0, 0), ("F", 0, 0),
-    ("oz", 1, 0), ("rz", 0, 2), ("ot", 0, 3), ("rx", 1, 0, 2), ("ot", 1, 2), ("ta", 0, 0), ("ot", 0, 1),
-    ("rz", 1, 1), ("rx", 0, 1, 0), ("rx", 1, 0, 1), ("TN", 0, 0, 0), ("tw",), ("rz", 1, 0), ("rz", 1, 3),
-    ("rx", 0, 1, 3), ("ot", 1, 1), ("F", 0, 1), ("ot", 0, 2), ("rx", 0, 1, 1), ("TF", 0, 0, 1), ("TF", 0, 0, 0),
-    ("TN", 0, 0, 1), ("Z", 0, 0, 2), ("rx", 1, 1, 2), ("ot", 1, 0), ("J", 0, 0, 0), ("Z", 0, 0, 3), ("ot", 1, 3),
-    ("B", 0, 0), ("rx", 1, 1, 1), ("rx", 0, 1, 2), ("J", 0, 0, 3), ("F", 1, 0), ("TF", 0, 1, 0), ("S", 0, 1, 1),
-    ("S", 0, 0, 1), ("J", 0, 0, 2), ("ta", 0, 1), ("S", 0, 1, 0), ("TN", 0, 1, 0), ("B", 0, 1), ("TN", 1, 0, 1),
-    ("rx", 1, 1, 0), ("S", 0, 0, 2), ("S", 0, 0, 3), ("ta", 1, 0), ("F", 1, 1), ("TF", 0, 1, 1), ("S", 0, 1, 3),
-    ("th", 0), ("ta", 1, 1), ("J", 0, 1, 0), ("rx", 1, 1, 3), ("J", 0, 1, 1), ("TF", 1, 0, 1), ("W", ("weight", 1)),
-    ("TN", 0, 1, 1), ("W", ("weight", 0)), ("B", 1, 0), ("S", 0, 1, 2), ("TF", 1, 1, 0), ("S", 1, 1, 0),
-    ("W", ("z", 0)), ("TN", 1, 0, 0), ("Z", 0, 1, 0), ("W", ("near", 0, 0)), ("th", 1), ("B", 1, 1), ("J", 0, 1, 3),
-    ("TF", 1, 0, 0), ("S", 1, 1, 1), ("Z", 1, 0, 2), ("Z", 1, 0, 3), ("TN", 1, 1, 0), ("Z", 0, 1, 1), ("J", 0, 0, 1),
-    ("W", ("near", 1, 0)), ("TF", 1, 1, 1), ("S", 1, 1, 2), ("S", 1, 1, 3), ("J", 0, 1, 2), ("W", ("far", 0, 0)),
-    ("C", 0, 1, 1), ("J", 1, 1, 0), ("G", 0, 1), ("C", 0, 1, 0), ("W", ("z", 1)), ("C", 0, 1, 3), ("S", 1, 0, 2),
-    ("TN", 1, 1, 1), ("J", 1, 1, 1), ("Z", 1, 1, 1), ("G", 1, 0), ("Z", 1, 1, 0), ("S", 1, 0, 0), ("PO", 0, 1),
-    ("W", ("far", 1, 0)), ("J", 1, 1, 2), ("J", 1, 1, 3), ("C", 0, 1, 2), ("S", 1, 0, 3), ("PO", 0, 0),
-    ("S", 1, 0, 1), ("C", 0, 0, 1), ("PO", 0, 3), ("W", ("near", 0, 1)), ("GS", 0, 1), ("G", 1, 1), ("J", 1, 0, 2),
-    ("C", 1, 1, 1), ("C", 0, 0, 3), ("RL", 1), ("GS", 1, 0), ("S", 0, 0, 0), ("C", 1, 1, 2), ("RL", 3),
-    ("W", ("near", 1, 1)), ("C", 1, 1, 0), ("RL", 2), ("PO", 0, 2), ("W", ("far", 0, 1)), ("C", 1, 1, 3),
-    ("J", 1, 0, 3), ("G", 0, 0), ("PO", 1, 1), ("J", 1, 0, 0), ("PO", 1, 2), ("RL", 0), ("C", 1, 0, 2),
-    ("C", 0, 0, 2), ("PO", 1, 0), ("J", 1, 0, 1), ("PO", 1, 3), ("GS", 1, 1), ("C", 1, 0, 3), ("FIN", 0, 2),
-    ("FIN", 0, 1), ("FIN", 1, 2), ("C", 0, 0, 0), ("FIN", 0, 3), ("FIN", 0, 0), ("GS", 0, 0), ("C", 1, 0, 0),
-    ("W", ("far", 1, 1)), ("FIN", 1, 0), ("C", 1, 0, 1), ("FIN", 1, 1), ("FIN", 1, 3),
-    ("W", ("middle", 0), ("middle", 1), ("out", 0), ("sum", 0, 0), ("term", 0, 1), ("term", 0, 0), ("sum", 0, 1), ("term", 1, 1), ("out", 1), ("sum", 1, 1), ("grad", 0, 1), ("term", 1, 0), ("grad", 1, 0), ("grad", 1, 1), ("sum", 1, 0), ("last",), ("grad", 0, 0)),
+    ("oz", 1, 1), ("ox", 0, 2), ("ox", 0, 0), ("ox", 0, 3), ("oz", 0, 2), ("su",), ("oz", 0, 1), ("sd",),
+    ("rz", 1, 1), ("ox", 1, 3), ("ox", 0, 1), ("oz", 0, 3), ("rx", 0, 0, 2), ("rx", 0, 0, 0), ("rz", 0, 2),
+    ("ox", 1, 2), ("oz", 0, 0), ("rx", 0, 0, 3), ("Fn", 0, 1), ("ox", 1, 1), ("oz", 1, 3), ("rz", 0, 1),
+    ("ot", 1, 1), ("rx", 1, 0, 3), ("ox", 1, 0), ("rz", 0, 3), ("rx", 0, 0, 1), ("tw",), ("oz", 1, 2), ("ot", 0, 2),
+    ("rz", 0, 0), ("rx", 1, 0, 2), ("F", 0, 1), ("TF", 0, 0, 1), ("rx", 1, 0, 1), ("oz", 1, 0), ("rz", 1, 3),
+    ("ot", 0, 3), ("ot", 0, 1), ("TN", 0, 0, 1), ("rx", 1, 1, 1), ("Fn", 0, 0), ("F", 0, 0), ("rz", 1, 2),
+    ("rx", 1, 0, 0), ("rx", 0, 1, 2), ("ot", 0, 0), ("th", 0), ("rx", 0, 1, 3), ("ot", 1, 3), ("rz", 1, 0),
+    ("Bn", 0, 1), ("ta", 0, 1), ("B", 0, 1), ("ot", 1, 2), ("rx", 0, 1, 1), ("Fn", 1, 1), ("rx", 0, 1, 0),
+    ("TF", 1, 0, 1), ("J", 0, 0, 3), ("Fn", 1, 0), ("Bn", 0, 0), ("ot", 1, 0), ("rx", 1, 1, 3), ("TN", 1, 0, 1),
+    ("J", 0, 0, 2), ("TF", 0, 0, 0), ("rx", 1, 1, 2), ("F", 1, 1), ("TF", 0, 1, 1), ("Z", 1, 0, 3), ("TN", 0, 1, 1),
+    ("Z", 0, 0, 3), ("S", 0, 1, 3), ("Z", 1, 0, 2), ("F", 1, 0), ("ta", 1, 0), ("rx", 1, 1, 0), ("Bn", 1, 1),
+    ("TF", 0, 1, 0), ("TN", 0, 1, 0), ("S", 0, 0, 3), ("S", 0, 1, 2), ("ta", 0, 0), ("Bn", 1, 0),
+    ("W", ("weight", 0)), ("Z", 0, 0, 2), ("S", 0, 1, 1), ("W", ("weight", 1)), ("S", 0, 0, 2), ("th", 1),
+    ("B", 1, 1), ("W", ("near", 0, 0)), ("J", 0, 1, 3), ("S", 0, 1, 0), ("B", 1, 0), ("TF", 1, 1, 0), ("Z", 0, 1, 0),
+    ("S", 1, 1, 1), ("W", ("z", 0)), ("B", 0, 0), ("TN", 1, 1, 0), ("TF", 1, 1, 1), ("S", 1, 1, 2), ("J", 0, 1, 2),
+    ("ta", 1, 1), ("Z", 1, 1, 0), ("Z", 1, 1, 1), ("W", ("near", 1, 0)), ("J", 0, 1, 1), ("S", 1, 1, 0),
+    ("W", ("far", 0, 0)), ("G", 1, 1), ("C", 0, 1, 3), ("J", 0, 1, 0), ("S", 1, 1, 3), ("TN", 1, 1, 1),
+    ("Z", 0, 1, 1), ("TF", 1, 0, 0), ("J", 1, 1, 1), ("S", 0, 0, 0), ("W", ("z", 1)), ("C", 0, 1, 2), ("C", 0, 1, 1),
+    ("S", 0, 0, 1), ("J", 1, 1, 2), ("G", 0, 1), ("J", 1, 1, 0), ("PO", 0, 3), ("S", 1, 0, 0), ("C", 0, 1, 0),
+    ("W", ("far", 1, 0)), ("TN", 0, 0, 0), ("J", 1, 1, 3), ("W", ("near", 0, 1)), ("S", 1, 0, 3), ("PO", 0, 1),
+    ("G", 0, 0), ("J", 0, 0, 0), ("C", 1, 1, 2), ("C", 1, 1, 1), ("J", 0, 0, 1), ("S", 1, 0, 2), ("C", 0, 0, 3),
+    ("S", 1, 0, 1), ("TN", 1, 0, 0), ("W", ("far", 0, 1)), ("PO", 0, 2), ("J", 1, 0, 0), ("C", 1, 1, 3),
+    ("C", 1, 1, 0), ("C", 0, 0, 2), ("W", ("near", 1, 1)), ("RL", 2), ("J", 1, 0, 3), ("PO", 0, 0), ("G", 1, 0),
+    ("PO", 1, 2), ("PO", 1, 1), ("J", 1, 0, 2), ("RL", 3), ("GS", 0, 0), ("C", 0, 0, 1), ("PO", 1, 3), ("PO", 1, 0),
+    ("J", 1, 0, 1), ("C", 0, 0, 0), ("FIN", 0, 2), ("W", ("far", 1, 1)), ("C", 1, 0, 0), ("GS", 1, 1), ("FIN", 0, 1),
+    ("GS", 0, 1), ("C", 1, 0, 2), ("FIN", 0, 0), ("FIN", 1, 2), ("C", 1, 0, 3), ("FIN", 0, 3), ("GS", 1, 0),
+    ("FIN", 1, 3), ("FIN", 1, 0), ("C", 1, 0, 1), ("FIN", 1, 1),
+    ("W", ("middle", 1), ("middle", 0), ("sum", 0, 0), ("out", 1), ("out", 0), ("term", 0, 1), ("term", 0, 0), ("sum", 0, 1), ("term", 1, 1), ("grad", 1, 1), ("sum", 1, 1), ("grad", 0, 1), ("term", 1, 0), ("grad", 0, 0), ("sum", 1, 0), ("last",), ("grad", 1, 0)),
 )
 
 
@@ -95,7 +101,7 @@
 
 def kernel(
     tok, cot, up, down, mask, out, gtok, gup, gdown,
-    held, held_t, raw, uall, dall, uall_t, dall_t, act, act_t, gpre, slope,
+    held, held_t, raw, uall, dall, uall_t, dall_t, act, act_t, gpre, slope, gact,
     term_send, term_recv, near_term, sum_send, sum_recv, base, z_term,
     half_send, half_recv, last_recv, z_send, z_recv,
     grad_own, grad_peer, grad_recv,
@@ -154,7 +160,7 @@
             if name == "far":
                 return remote(held.at[which, NEAR[axis], at], held.at[which, FAR[axis], at], key, axis + "3")
             if name == "term":
-                target = axis + ("1" if (which, slot) == (0, 0) else "3")
+                target = axis + ("1" if passed(which, slot, j) else "3")
                 return remote(term_send.at[which, a, at], term_recv.at[which, a, at], key, target)
             return remote(sum_send.at[which, a, at], sum_recv.at[which, a, at], key, axis + "1")
         which, j = rest
@@ -206,9 +212,6 @@
         dall[pl.ds(0, G), pl.ds(pl.multiple_of(k * G, G), G)] = (raw[1, k].astype(F32) * factor).astype(BF16)
         return carry
 
-    def wide(which, at):
-        return jnp.concatenate([held[which, level, at] for level in range(LEVELS)], axis=1)
-
     def tile(slot, t):
         return pl.ds(slot * ROWS + t * TILE, TILE)
 
@@ -263,20 +266,40 @@
     def turn_act(slot, t):
         act_t[:, tile(slot, t)] = act[tile(slot, t), :].T
 
-    def inputs(which, slot, t):
+    def near_inputs(which, slot, t):
         if slot == 0 and ("own", which) not in copied:
             copied.add(("own", which))
             own[which].wait()
         for j in range(t * PER_TILE, (t + 1) * PER_TILE):
             need(("z3" if slot else "z1", which, j))
+
+    def far_inputs(which, slot, t):
+        for j in range(t * PER_TILE, (t + 1) * PER_TILE):
             for axis in "xy":
                 need(("far", axis, which, slot, j))
 
+    def partial(which, at, weights):
+        early = jnp.concatenate([held[which, level, at] for level in (0, 1, 2)], axis=1)
+        total = jnp.dot(early, weights[pl.ds(0, 3 * G), :], preferred_element_type=F32)
+        return total + jnp.dot(held[which, 4, at], weights[pl.ds(4 * G, G), :], preferred_element_type=F32)
+
+    def rest(which, at, weights):
+        total = jnp.dot(held[which, 3, at], weights[pl.ds(3 * G, G), :], preferred_element_type=F32)
+        return total + jnp.dot(held[which, 5, at], weights[pl.ds(5 * G, G), :], preferred_element_type=F32)
+
+    def forward_near(slot, t):
+        near_inputs(0, slot, t)
+        need(("weight", 0))
+        slope[tile(slot, t), :] = partial(0, tile(slot, t), uall)
+
+    def backward_near(slot, t):
+        near_inputs(1, slot, t)
+        gact[tile(slot, t), :] = partial(1, tile(slot, t), dall_t)
+
     def forward(slot, t):
-        inputs(0, slot, t)
-        need(("weight", 0), ("weight", 1))
+        far_inputs(0, slot, t)
         at = tile(slot, t)
-        pre = jnp.dot(wide(0, at), uall[...], preferred_element_type=F32)
+        pre = slope[at, :] + rest(0, at, uall)
         square = pre * pre
         tanh = jnp.tanh(SCALE * pre * (1.0 + CUBE * square))
         cdf = 0.5 + 0.5 * tanh
@@ -284,10 +307,9 @@
         slope[at, :] = cdf + (0.5 * SCALE) * pre * (1.0 - tanh * tanh) * (1.0 + (3.0 * CUBE) * square)
 
     def backward(slot, t):
-        inputs(1, slot, t)
+        far_inputs(1, slot, t)
         at = tile(slot, t)
-        gact = jnp.dot(wide(1, at), dall_t[...], preferred_element_type=F32)
-        gpre[at, :] = (gact * slope[at, :]).astype(BF16)
+        gpre[at, :] = ((gact[at, :] + rest(1, at, dall_t)) * slope[at, :]).astype(BF16)
 
     def product(which, slot, t, level):
         if which:
@@ -295,6 +317,7 @@
         return jnp.dot(act[tile(slot, t), :], dall[:, columns(level)], preferred_element_type=F32)
 
     def far_terms(which, slot, t):
+        need(("weight", 1))
         for a, axis in enumerate("xy"):
             term_send[which, a, tile(slot, t)] = product(which, slot, t, FAR[axis]).astype(BF16)
 
@@ -317,7 +340,7 @@
         at = rows(slot, j)
         for a, axis in enumerate("xy"):
             total = near_term[which, a, at]
-            if (which, slot) != (0, 0):
+            if not passed(which, slot, j):
                 need(("term", axis, which, slot, j))
                 total = total + term_recv[which, a, at].astype(F32)
             sum_send[which, a, at] = total.astype(BF16)
@@ -347,7 +370,7 @@
     def finish(which, j):
         need(("out1", which, j), ("out3", which, j))
         total = base[which, rows(0, j)] + z_recv[which, rows(0, j)].astype(F32) + z_recv[which, rows(1, j)].astype(F32)
-        if which == 0:
+        if passed(which, 0, j):
             need(("last", "x", j), ("last", "y", j))
             total = total + last_recv[0, piece(j)].astype(F32) + last_recv[1, piece(j)].astype(F32)
         (gtok if which else out)[piece(j), :] = total.astype(BF16)
@@ -383,9 +406,20 @@
 
     def finish_sends(*names):
         for name in names:
-            sent.add(name)
+            sent.update([(name[0], j) for j in PASSED] if name[0] == "last" else [name])
             if name[0] in ("weight", "grad"):
                 transfer(name).wait_send()
+            elif name[0] == "last":
+                for j in PASSED:
+                    span = pl.ds(0, 2 * PART)
+                    pltpu.make_async_remote_copy(
+                        src_ref=held.at[0, 0, span],
+                        dst_ref=held.at[0, 0, span],
+                        send_sem=sends.at[FAMILIES["last", j]],
+                        recv_sem=recvs.at[0],
+                        device_id=place["z1"],
+                        device_id_type=MESH,
+                    ).wait_send()
             else:
                 pltpu.make_async_remote_copy(
                     src_ref=held.at[0, 0],
@@ -399,7 +433,7 @@
     steps = {
         "W": finish_sends,
         "oz": own_z, "ox": own_xy, "rz": relay_z, "ot": other, "rx": relay_xy, "su": mask_up, "sd": mask_down,
-        "tw": turn_weights, "th": turn_held, "ta": turn_act, "F": forward, "B": backward, "TF": far_terms,
+        "tw": turn_weights, "th": turn_held, "ta": turn_act, "F": forward, "B": backward, "Fn": forward_near, "Bn": backward_near, "TF": far_terms,
         "TN": near_terms, "S": send_term, "RL": hand_on, "J": join, "C": collect, "Z": plain, "PO": pass_on,
         "FIN": finish, "G": grads, "GS": grads_sum,
     }
@@ -456,6 +490,7 @@
             pltpu.VMEM((both, 2 * G), BF16),
             pltpu.VMEM((2 * G, both), BF16),
             pltpu.VMEM((both, 2 * G), BF16),
+            pltpu.VMEM((both, 2 * G), F32),
             pltpu.VMEM((both, 2 * G), F32),
             pltpu.VMEM((2, 2, both, G), BF16),
             pltpu.VMEM((2, 2, both, G), BF16),

time: 67.5 us -> 66.8 us (0.990)
  Pallas kernels: 66.7 us -> 66 us
where the time goes in v2:
time: 66.8 us; the launch traced here: 66.7 us
  Pallas kernels  66 us (99%)
    pallas_call x1, Pallas kernels, shards(): pl.pallas_call(kernel, out_shape=tuple((pltpu.VMEM(a.shape, a.dtype) for...  64.1 us
    pallas_call x1, Pallas kernels, shards(): pl.pallas_call(hand_out, out_shape=result, in_specs=[anywhere] * 4, out_s...  1.9 us

profile of v2, /device:TPU:0, one launch (start us, length us, event | category | flops | bytes accessed | tf_op | source)
XLA Modules:
  0.0 66.7 jit_solution(6595040101596029678)
XLA Ops:
  0.6 64.1 %shard_map.84 = (bf16[512,256]{1,0:T(8,128)(2,1)S(1)}, bf16[512,256]{1,0:T(8,128)(2,1)S(1)}, f32[6,256,256]{2,1,0:T(8,128)S(1)}, f32[6,256,256]{2,1,0:T(8,128)S(1)}) custom-call(bf16[512,256]{1,0:T(8,128)(2,1)} %tok.1, bf16[512,256]{1,0:T(8,128)(2,1)} %cot.1, bf16[6,256,256]{2,1,0:T(8,128)(2,1)} %bitcast.4, bf16[6,256,256]{2,1,0:T(8,128)(2,1)} %bitcast.5, ...), custom_call_target="tpu_custom_call" | custom-call | tf_op jit(solution)/shard_map/pallas_call | solution.py:477
  64.8 1.9 %shard_map.85 = (bf16[512,256]{1,0:T(8,128)(2,1)}, bf16[512,256]{1,0:T(8,128)(2,1)}, f32[6,256,256]{2,1,0:T(8,128)}, f32[6,256,256]{2,1,0:T(8,128)}) custom-call(bf16[512,256]{1,0:T(8,128)(2,1)S(1)} %get-tuple-element.12.refs_0_, bf16[512,256]{1,0:T(8,128)(2,1)S(1)} %get-tuple-element.13.refs_1_, f32[6,256,256]{2,1,0:T(8,128)S(1)} %get-tuple-element.14.refs_2_, ...), custom_call_target="tpu_custom_call" | custom-call | tf_op jit(solution)/shard_map/pallas_call | solution.py:519

commit v3 on v2

--- a/solution.py
+++ b/solution.py
@@ -1,4 +1,4 @@
-import functools
+import collections
 import math
 
 import jax
@@ -40,6 +40,9 @@
         ]
         keys += [("weight", which)] + [("grad", which, k) for k in range(LEVELS // THIRDS)]
     keys += [("last", axis, j) for axis in "xy" for j in PASSED]
+    moved = [(axis, level, which, j) for axis in "xy" for level in "nf" for which, j in MOVED]
+    keys += [("hop", *rest) for rest in moved] + [("land", *rest) for rest in moved]
+    keys = [k for k in keys if not (k[0] in ("near", "far") and k[3] == 1 and (k[2], k[4]) in MOVED)]
     return {key: n for n, key in enumerate(keys)}
 
 
@@ -53,45 +56,51 @@
         return key
     if name in ("near", "far", "term", "sum"):
         return name, key[2], key[3]
-    if name == "last":
-        return name, key[2]
+    if name in ("last", "hop", "land"):
+        return (name,)
     return {"z1": "z", "z3": "z", "zr": "middle", "half": "middle", "out1": "out", "out3": "out"}[name], key[1]
 
 
 PASSED = (2, 3)
+MOVED = ((1, 0), (1, 2))
 NUMBER = numbering()
 COPIES = len(NUMBER)
-FAMILIES = {name: n for n, name in enumerate(dict.fromkeys(family(key) for key in NUMBER))}
+SIZES = collections.Counter(family(key) for key in NUMBER)
+FAMILIES = {name: n for n, name in enumerate(SIZES)}
 
 ORDER = (
-    ("oz", 1, 1), ("ox", 0, 2), ("ox", 0, 0), ("ox", 0, 3), ("oz", 0, 2), ("su",), ("oz", 0, 1), ("sd",),
-    ("rz", 1, 1), ("ox", 1, 3), ("ox", 0, 1), ("oz", 0, 3), ("rx", 0, 0, 2), ("rx", 0, 0, 0), ("rz", 0, 2),
-    ("ox", 1, 2), ("oz", 0, 0), ("rx", 0, 0, 3), ("Fn", 0, 1), ("ox", 1, 1), ("oz", 1, 3), ("rz", 0, 1),
-    ("ot", 1, 1), ("rx", 1, 0, 3), ("ox", 1, 0), ("rz", 0, 3), ("rx", 0, 0, 1), ("tw",), ("oz", 1, 2), ("ot", 0, 2),
-    ("rz", 0, 0), ("rx", 1, 0, 2), ("F", 0, 1), ("TF", 0, 0, 1), ("rx", 1, 0, 1), ("oz", 1, 0), ("rz", 1, 3),
-    ("ot", 0, 3), ("ot", 0, 1), ("TN", 0, 0, 1), ("rx", 1, 1, 1), ("Fn", 0, 0), ("F", 0, 0), ("rz", 1, 2),
-    ("rx", 1, 0, 0), ("rx", 0, 1, 2), ("ot", 0, 0), ("th", 0), ("rx", 0, 1, 3), ("ot", 1, 3), ("rz", 1, 0),
-    ("Bn", 0, 1), ("ta", 0, 1), ("B", 0, 1), ("ot", 1, 2), ("rx", 0, 1, 1), ("Fn", 1, 1), ("rx", 0, 1, 0),
-    ("TF", 1, 0, 1), ("J", 0, 0, 3), ("Fn", 1, 0), ("Bn", 0, 0), ("ot", 1, 0), ("rx", 1, 1, 3), ("TN", 1, 0, 1),
-    ("J", 0, 0, 2), ("TF", 0, 0, 0), ("rx", 1, 1, 2), ("F", 1, 1), ("TF", 0, 1, 1), ("Z", 1, 0, 3), ("TN", 0, 1, 1),
-    ("Z", 0, 0, 3), ("S", 0, 1, 3), ("Z", 1, 0, 2), ("F", 1, 0), ("ta", 1, 0), ("rx", 1, 1, 0), ("Bn", 1, 1),
-    ("TF", 0, 1, 0), ("TN", 0, 1, 0), ("S", 0, 0, 3), ("S", 0, 1, 2), ("ta", 0, 0), ("Bn", 1, 0),
-    ("W", ("weight", 0)), ("Z", 0, 0, 2), ("S", 0, 1, 1), ("W", ("weight", 1)), ("S", 0, 0, 2), ("th", 1),
-    ("B", 1, 1), ("W", ("near", 0, 0)), ("J", 0, 1, 3), ("S", 0, 1, 0), ("B", 1, 0), ("TF", 1, 1, 0), ("Z", 0, 1, 0),
-    ("S", 1, 1, 1), ("W", ("z", 0)), ("B", 0, 0), ("TN", 1, 1, 0), ("TF", 1, 1, 1), ("S", 1, 1, 2), ("J", 0, 1, 2),
-    ("ta", 1, 1), ("Z", 1, 1, 0), ("Z", 1, 1, 1), ("W", ("near", 1, 0)), ("J", 0, 1, 1), ("S", 1, 1, 0),
-    ("W", ("far", 0, 0)), ("G", 1, 1), ("C", 0, 1, 3), ("J", 0, 1, 0), ("S", 1, 1, 3), ("TN", 1, 1, 1),
-    ("Z", 0, 1, 1), ("TF", 1, 0, 0), ("J", 1, 1, 1), ("S", 0, 0, 0), ("W", ("z", 1)), ("C", 0, 1, 2), ("C", 0, 1, 1),
-    ("S", 0, 0, 1), ("J", 1, 1, 2), ("G", 0, 1), ("J", 1, 1, 0), ("PO", 0, 3), ("S", 1, 0, 0), ("C", 0, 1, 0),
-    ("W", ("far", 1, 0)), ("TN", 0, 0, 0), ("J", 1, 1, 3), ("W", ("near", 0, 1)), ("S", 1, 0, 3), ("PO", 0, 1),
-    ("G", 0, 0), ("J", 0, 0, 0), ("C", 1, 1, 2), ("C", 1, 1, 1), ("J", 0, 0, 1), ("S", 1, 0, 2), ("C", 0, 0, 3),
-    ("S", 1, 0, 1), ("TN", 1, 0, 0), ("W", ("far", 0, 1)), ("PO", 0, 2), ("J", 1, 0, 0), ("C", 1, 1, 3),
-    ("C", 1, 1, 0), ("C", 0, 0, 2), ("W", ("near", 1, 1)), ("RL", 2), ("J", 1, 0, 3), ("PO", 0, 0), ("G", 1, 0),
-    ("PO", 1, 2), ("PO", 1, 1), ("J", 1, 0, 2), ("RL", 3), ("GS", 0, 0), ("C", 0, 0, 1), ("PO", 1, 3), ("PO", 1, 0),
-    ("J", 1, 0, 1), ("C", 0, 0, 0), ("FIN", 0, 2), ("W", ("far", 1, 1)), ("C", 1, 0, 0), ("GS", 1, 1), ("FIN", 0, 1),
-    ("GS", 0, 1), ("C", 1, 0, 2), ("FIN", 0, 0), ("FIN", 1, 2), ("C", 1, 0, 3), ("FIN", 0, 3), ("GS", 1, 0),
-    ("FIN", 1, 3), ("FIN", 1, 0), ("C", 1, 0, 1), ("FIN", 1, 1),
-    ("W", ("middle", 1), ("middle", 0), ("sum", 0, 0), ("out", 1), ("out", 0), ("term", 0, 1), ("term", 0, 0), ("sum", 0, 1), ("term", 1, 1), ("grad", 1, 1), ("sum", 1, 1), ("grad", 0, 1), ("term", 1, 0), ("grad", 0, 0), ("sum", 1, 0), ("last",), ("grad", 1, 0)),
+    ("oz", 0, 3), ("ox", 0, 3), ("ox", 1, 0), ("oz", 0, 2), ("oz", 0, 1), ("su",), ("oz", 1, 1), ("ox", 1, 2),
+    ("ox", 0, 2), ("sd",), ("ox", 0, 1), ("rx", 0, 0, 3), ("ox", 0, 0), ("oz", 0, 0), ("rx", 1, 0, 0), ("ox", 1, 3),
+    ("rz", 0, 3), ("rz", 0, 2), ("rx", 1, 0, 2), ("rz", 0, 1), ("oz", 1, 3), ("ox", 1, 1), ("h1", "x", "n", 1, 2),
+    ("rx", 0, 0, 2), ("Fn", 0, 1), ("rz", 0, 0), ("rz", 1, 1), ("rx", 0, 0, 1), ("oz", 1, 2), ("h1", "y", "f", 1, 0),
+    ("tw",), ("ot", 0, 3), ("h1", "y", "f", 1, 2), ("h1", "x", "f", 1, 2), ("rx", 0, 0, 0), ("F", 0, 1),
+    ("rz", 1, 3), ("ot", 0, 2), ("rx", 1, 0, 3), ("h1", "x", "n", 1, 0), ("ot", 0, 1), ("h1", "x", "f", 1, 0),
+    ("Fn", 0, 0), ("rx", 1, 0, 1), ("h1", "y", "n", 1, 2), ("h1", "y", "n", 1, 0), ("ot", 0, 0), ("TF", 0, 0, 1),
+    ("oz", 1, 0), ("rx", 0, 1, 3), ("TN", 0, 0, 1), ("F", 0, 0), ("TF", 0, 0, 0), ("rx", 0, 1, 2), ("rz", 1, 2),
+    ("ot", 1, 1), ("Bn", 0, 1), ("h2", "x", "n", 1, 2), ("B", 0, 1), ("TF", 1, 0, 1), ("rx", 0, 1, 1),
+    ("TN", 0, 0, 0), ("ot", 1, 3), ("S", 0, 0, 2), ("TN", 1, 0, 1), ("S", 1, 0, 2), ("h2", "y", "f", 1, 2),
+    ("Fn", 1, 1), ("ta", 0, 1), ("J", 0, 0, 2), ("rx", 0, 1, 0), ("F", 1, 1), ("TF", 0, 1, 1), ("S", 0, 1, 2),
+    ("h2", "y", "f", 1, 0), ("S", 0, 0, 3), ("rx", 1, 1, 1), ("h2", "x", "n", 1, 0), ("J", 0, 0, 3), ("Fn", 1, 0),
+    ("TN", 0, 1, 1), ("S", 0, 1, 3), ("rz", 1, 0), ("Bn", 0, 0), ("ta", 0, 0), ("W", ("weight", 0)),
+    ("h2", "x", "f", 1, 0), ("h2", "x", "f", 1, 2), ("B", 0, 0), ("h2", "y", "n", 1, 0), ("W", ("weight", 1)),
+    ("TF", 1, 0, 0), ("rx", 1, 1, 3), ("F", 1, 0), ("W", ("near", 0, 0)), ("J", 1, 0, 2), ("W", ("z", 0)),
+    ("h2", "y", "n", 1, 2), ("Z", 0, 0, 2), ("TF", 0, 1, 0), ("ta", 1, 0), ("ot", 1, 2), ("S", 0, 1, 0),
+    ("Z", 0, 0, 3), ("J", 0, 1, 2), ("W", ("near", 1, 0)), ("Z", 1, 0, 3), ("ta", 1, 1), ("ot", 1, 0),
+    ("TN", 0, 1, 0), ("th", 0), ("Z", 0, 1, 0), ("Bn", 1, 0), ("Z", 1, 0, 2), ("B", 1, 0), ("TF", 1, 1, 0),
+    ("S", 1, 1, 1), ("TN", 1, 1, 0), ("J", 0, 1, 3), ("W", ("far", 0, 0)), ("S", 1, 1, 0), ("Bn", 1, 1), ("B", 1, 1),
+    ("TF", 1, 1, 1), ("J", 0, 1, 0), ("S", 1, 1, 3), ("Z", 1, 1, 1), ("S", 0, 1, 1), ("S", 1, 1, 2),
+    ("W", ("far", 1, 0)), ("S", 0, 0, 1), ("Z", 1, 1, 0), ("W", ("hop",)), ("TN", 1, 1, 1), ("W", ("near", 0, 1)),
+    ("S", 1, 0, 3), ("J", 1, 1, 1), ("W", ("z", 1)), ("G", 1, 1), ("J", 1, 1, 0), ("C", 0, 1, 0), ("S", 0, 0, 0),
+    ("J", 1, 1, 3), ("Z", 0, 1, 1), ("G", 1, 0), ("C", 0, 1, 2), ("C", 1, 1, 1), ("J", 0, 1, 1), ("C", 0, 1, 3),
+    ("J", 1, 1, 2), ("th", 1), ("S", 1, 0, 0), ("S", 1, 0, 1), ("C", 1, 1, 0), ("C", 1, 1, 3), ("G", 0, 1),
+    ("PO", 0, 2), ("J", 0, 0, 1), ("PO", 0, 0), ("TN", 1, 0, 0), ("W", ("far", 0, 1)), ("J", 1, 0, 3),
+    ("C", 0, 1, 1), ("RL", 2), ("C", 1, 1, 2), ("J", 0, 0, 0), ("PO", 1, 1), ("PO", 0, 3), ("G", 0, 0), ("PO", 1, 3),
+    ("J", 1, 0, 1), ("PO", 1, 0), ("C", 1, 0, 2), ("RL", 3), ("PO", 0, 1), ("J", 1, 0, 0), ("PO", 1, 2),
+    ("GS", 1, 0), ("GS", 0, 1), ("C", 0, 0, 2), ("GS", 1, 1), ("W", ("far", 1, 1)), ("C", 0, 0, 1), ("C", 0, 0, 0),
+    ("C", 1, 0, 3), ("W", ("land",)), ("FIN", 0, 2), ("FIN", 0, 0), ("C", 0, 0, 3), ("FIN", 1, 3), ("C", 1, 0, 1),
+    ("FIN", 1, 1), ("FIN", 0, 3), ("GS", 0, 0), ("FIN", 1, 2), ("C", 1, 0, 0), ("W", ("near", 1, 1)), ("FIN", 1, 0),
+    ("FIN", 0, 1),
+    ("W", ("middle", 0), ("middle", 1), ("term", 0, 0), ("term", 1, 0), ("sum", 0, 0), ("term", 0, 1), ("sum", 1, 0), ("out", 0), ("sum", 0, 1), ("out", 1), ("term", 1, 1), ("sum", 1, 1), ("grad", 1, 1), ("grad", 1, 0), ("grad", 0, 1), ("last",), ("grad", 0, 0)),
 )
 
 
@@ -103,7 +112,7 @@
     tok, cot, up, down, mask, out, gtok, gup, gdown,
     held, held_t, raw, uall, dall, uall_t, dall_t, act, act_t, gpre, slope, gact,
     term_send, term_recv, near_term, sum_send, sum_recv, base, z_term,
-    half_send, half_recv, last_recv, z_send, z_recv,
+    half_send, half_recv, last_recv, hops, z_send, z_recv,
     grad_own, grad_peer, grad_recv,
     sends, recvs, local,
 ):
@@ -151,6 +160,13 @@
         if name == "last":
             a, j = "xy".index(rest[0]), rest[1]
             return remote(term_recv.at[0, a, rows(0, j)], last_recv.at[a, piece(j)], key, rest[0] + "3")
+        if name in ("hop", "land"):
+            axis, level, which, j = rest
+            n, group = "nf".index(level), (NEAR if level == "n" else FAR)[axis]
+            room = hops.at[n, "xy".index(axis), pl.ds(MOVED.index((which, j)) * PART, PART)]
+            if name == "hop":
+                return remote(held.at[which, group, rows(0, j)], room, key, ("z1", "z3")[n])
+            return remote(room, held.at[which, group, rows(1, j)], key, ("z3", "z1")[n])
         if name in ("near", "far", "term", "sum"):
             axis, which, slot, j = rest
             a, at = "xy".index(axis), rows(slot, j)
@@ -227,12 +243,21 @@
 
     def other(which, j):
         need(("zr", which, j))
-        send(("near", "x", which, 1, j), ("near", "y", which, 1, j))
+        if (which, j) not in MOVED:
+            send(("near", "x", which, 1, j), ("near", "y", which, 1, j))
 
     def relay_xy(which, slot, j):
         for axis in "xy":
             need(("near", axis, which, slot, j))
             send(("far", axis, which, slot, j))
+
+    def hop(axis, level, which, j):
+        need(("near" if level == "n" else "far", axis, which, 0, j))
+        send(("hop", axis, level, which, j))
+
+    def land(axis, level, which, j):
+        need(("hop", axis, level, which, j))
+        send(("land", axis, level, which, j))
 
     def mask_up():
         loads[0].wait()
@@ -272,11 +297,13 @@
             own[which].wait()
         for j in range(t * PER_TILE, (t + 1) * PER_TILE):
             need(("z3" if slot else "z1", which, j))
+            if slot and (which, j) in MOVED:
+                need(("land", "x", "n", which, j), ("land", "y", "n", which, j))
 
     def far_inputs(which, slot, t):
         for j in range(t * PER_TILE, (t + 1) * PER_TILE):
             for axis in "xy":
-                need(("far", axis, which, slot, j))
+                need(("land", axis, "f", which, j) if slot and (which, j) in MOVED else ("far", axis, which, slot, j))
 
     def partial(which, at, weights):
         early = jnp.concatenate([held[which, level, at] for level in (0, 1, 2)], axis=1)
@@ -406,24 +433,14 @@
 
     def finish_sends(*names):
         for name in names:
-            sent.update([(name[0], j) for j in PASSED] if name[0] == "last" else [name])
+            sent.add(name)
             if name[0] in ("weight", "grad"):
                 transfer(name).wait_send()
-            elif name[0] == "last":
-                for j in PASSED:
-                    span = pl.ds(0, 2 * PART)
-                    pltpu.make_async_remote_copy(
-                        src_ref=held.at[0, 0, span],
-                        dst_ref=held.at[0, 0, span],
-                        send_sem=sends.at[FAMILIES["last", j]],
-                        recv_sem=recvs.at[0],
-                        device_id=place["z1"],
-                        device_id_type=MESH,
-                    ).wait_send()
             else:
+                span = pl.ds(0, SIZES[name] * PART)
                 pltpu.make_async_remote_copy(
-                    src_ref=held.at[0, 0],
-                    dst_ref=held.at[0, 0],
+                    src_ref=held.at[0, 0, span],
+                    dst_ref=held.at[0, 0, span],
                     send_sem=sends.at[FAMILIES[name]],
                     recv_sem=recvs.at[0],
                     device_id=place["z1"],
@@ -433,7 +450,7 @@
     steps = {
         "W": finish_sends,
         "oz": own_z, "ox": own_xy, "rz": relay_z, "ot": other, "rx": relay_xy, "su": mask_up, "sd": mask_down,
-        "tw": turn_weights, "th": turn_held, "ta": turn_act, "F": forward, "B": backward, "Fn": forward_near, "Bn": backward_near, "TF": far_terms,
+        "tw": turn_weights, "th": turn_held, "ta": turn_act, "F": forward, "B": backward, "h1": hop, "h2": land, "Fn": forward_near, "Bn": backward_near, "TF": far_terms,
         "TN": near_terms, "S": send_term, "RL": hand_on, "J": join, "C": collect, "Z": plain, "PO": pass_on,
         "FIN": finish, "G": grads, "GS": grads_sum,
     }
@@ -502,6 +519,7 @@
             pltpu.VMEM((2, ROWS, G), BF16),
             pltpu.VMEM((2, ROWS, G), BF16),
             pltpu.VMEM((2, ROWS, G), BF16),
+            pltpu.VMEM((2, 2, len(MOVED) * PART, G), BF16),
             pltpu.VMEM((2, both, G), BF16),
             pltpu.VMEM((2, both, G), BF16),
             pltpu.VMEM((2, LEVELS, G, G), F32),

time: 66.8 us -> 65.1 us (0.975)
  Pallas kernels: 66 us -> 64.3 us
    pallas_call x1, Pallas kernels: 64.1 us -> 62.4 us  [shards(): pl.pallas_call(kernel, out_shape=tuple((pltpu.VMEM(a.shape, a.dtype) for...]
where the time goes in v3:
time: 65.1 us; the launch traced here: 65 us
  Pallas kernels  64.3 us (99%)
    pallas_call x1, Pallas kernels, shards(): pl.pallas_call(kernel, out_shape=tuple((pltpu.VMEM(a.shape, a.dtype) for...  62.4 us
    pallas_call x1, Pallas kernels, shards(): pl.pallas_call(hand_out, out_shape=result, in_specs=[anywhere] * 4, out_s...  1.9 us

profile of v3, /device:TPU:0, one launch (start us, length us, event | category | flops | bytes accessed | tf_op | source)
XLA Modules:
  0.0 65.0 jit_solution(12221871726986129593)
XLA Ops:
  0.6 62.4 %shard_map.84 = (bf16[512,256]{1,0:T(8,128)(2,1)S(1)}, bf16[512,256]{1,0:T(8,128)(2,1)S(1)}, f32[6,256,256]{2,1,0:T(8,128)S(1)}, f32[6,256,256]{2,1,0:T(8,128)S(1)}) custom-call(bf16[512,256]{1,0:T(8,128)(2,1)} %tok.1, bf16[512,256]{1,0:T(8,128)(2,1)} %cot.1, bf16[6,256,256]{2,1,0:T(8,128)(2,1)} %bitcast.4, bf16[6,256,256]{2,1,0:T(8,128)(2,1)} %bitcast.5, ...), custom_call_target="tpu_custom_call" | custom-call | tf_op jit(solution)/shard_map/pallas_call | solution.py:494
  63.1 1.9 %shard_map.85 = (bf16[512,256]{1,0:T(8,128)(2,1)}, bf16[512,256]{1,0:T(8,128)(2,1)}, f32[6,256,256]{2,1,0:T(8,128)}, f32[6,256,256]{2,1,0:T(8,128)}) custom-call(bf16[512,256]{1,0:T(8,128)(2,1)S(1)} %get-tuple-element.12.refs_0_, bf16[512,256]{1,0:T(8,128)(2,1)S(1)} %get-tuple-element.13.refs_1_, f32[6,256,256]{2,1,0:T(8,128)S(1)} %get-tuple-element.14.refs_2_, ...), custom_call_target="tpu_custom_call" | custom-call | tf_op jit(solution)/shard_map/pallas_call | solution.py:537

commit v4 on v3

--- a/solution.py
+++ b/solution.py
@@ -21,8 +21,9 @@
 G = 256
 LEVELS = 6
 WIDE = LEVELS * G
-NEAR = {"x": 4, "y": 2}
-FAR = {"x": 5, "y": 3}
+LEVEL = (0, 1, 2, 4, 3, 5)
+NEAR = {"x": 3, "y": 2}
+FAR = {"x": 5, "y": 4}
 SCALE = math.sqrt(2.0 / math.pi)
 CUBE = 0.044715
 
@@ -61,46 +62,58 @@
     return {"z1": "z", "z3": "z", "zr": "middle", "half": "middle", "out1": "out", "out3": "out"}[name], key[1]
 
 
+def arrival(key):
+    name = key[0]
+    if name in ("near", "far", "term", "sum"):
+        return name, *key[2:]
+    if name in ("out1", "out3"):
+        return "out", *key[1:]
+    if name in ("last", "land"):
+        return name, *key[2:]
+    return key
+
+
 PASSED = (2, 3)
 MOVED = ((1, 0), (1, 2))
 NUMBER = numbering()
-COPIES = len(NUMBER)
+ARRIVALS = collections.Counter(arrival(key) for key in NUMBER)
+LANDINGS = {name: n for n, name in enumerate(ARRIVALS)}
 SIZES = collections.Counter(family(key) for key in NUMBER)
 FAMILIES = {name: n for n, name in enumerate(SIZES)}
 
+S_OX, S_OZ, S_RZ, S_OT, S_RX, S_H1, S_H2, S_SU, S_SD, S_TW, S_TH, S_TA, S_FN, S_F, \
+    S_BN, S_B, S_TF, S_TN, S_S, S_RL, S_J, S_C, S_Z, S_PO, S_FIN, S_G, S_GS, S_W = range(28)
+X, Y, NR, FR = "x", "y", "n", "f"
 ORDER = (
-    ("oz", 0, 3), ("ox", 0, 3), ("ox", 1, 0), ("oz", 0, 2), ("oz", 0, 1), ("su",), ("oz", 1, 1), ("ox", 1, 2),
-    ("ox", 0, 2), ("sd",), ("ox", 0, 1), ("rx", 0, 0, 3), ("ox", 0, 0), ("oz", 0, 0), ("rx", 1, 0, 0), ("ox", 1, 3),
-    ("rz", 0, 3), ("rz", 0, 2), ("rx", 1, 0, 2), ("rz", 0, 1), ("oz", 1, 3), ("ox", 1, 1), ("h1", "x", "n", 1, 2),
-    ("rx", 0, 0, 2), ("Fn", 0, 1), ("rz", 0, 0), ("rz", 1, 1), ("rx", 0, 0, 1), ("oz", 1, 2), ("h1", "y", "f", 1, 0),
-    ("tw",), ("ot", 0, 3), ("h1", "y", "f", 1, 2), ("h1", "x", "f", 1, 2), ("rx", 0, 0, 0), ("F", 0, 1),
-    ("rz", 1, 3), ("ot", 0, 2), ("rx", 1, 0, 3), ("h1", "x", "n", 1, 0), ("ot", 0, 1), ("h1", "x", "f", 1, 0),
-    ("Fn", 0, 0), ("rx", 1, 0, 1), ("h1", "y", "n", 1, 2), ("h1", "y", "n", 1, 0), ("ot", 0, 0), ("TF", 0, 0, 1),
-    ("oz", 1, 0), ("rx", 0, 1, 3), ("TN", 0, 0, 1), ("F", 0, 0), ("TF", 0, 0, 0), ("rx", 0, 1, 2), ("rz", 1, 2),
-    ("ot", 1, 1), ("Bn", 0, 1), ("h2", "x", "n", 1, 2), ("B", 0, 1), ("TF", 1, 0, 1), ("rx", 0, 1, 1),
-    ("TN", 0, 0, 0), ("ot", 1, 3), ("S", 0, 0, 2), ("TN", 1, 0, 1), ("S", 1, 0, 2), ("h2", "y", "f", 1, 2),
-    ("Fn", 1, 1), ("ta", 0, 1), ("J", 0, 0, 2), ("rx", 0, 1, 0), ("F", 1, 1), ("TF", 0, 1, 1), ("S", 0, 1, 2),
-    ("h2", "y", "f", 1, 0), ("S", 0, 0, 3), ("rx", 1, 1, 1), ("h2", "x", "n", 1, 0), ("J", 0, 0, 3), ("Fn", 1, 0),
-    ("TN", 0, 1, 1), ("S", 0, 1, 3), ("rz", 1, 0), ("Bn", 0, 0), ("ta", 0, 0), ("W", ("weight", 0)),
-    ("h2", "x", "f", 1, 0), ("h2", "x", "f", 1, 2), ("B", 0, 0), ("h2", "y", "n", 1, 0), ("W", ("weight", 1)),
-    ("TF", 1, 0, 0), ("rx", 1, 1, 3), ("F", 1, 0), ("W", ("near", 0, 0)), ("J", 1, 0, 2), ("W", ("z", 0)),
-    ("h2", "y", "n", 1, 2), ("Z", 0, 0, 2), ("TF", 0, 1, 0), ("ta", 1, 0), ("ot", 1, 2), ("S", 0, 1, 0),
-    ("Z", 0, 0, 3), ("J", 0, 1, 2), ("W", ("near", 1, 0)), ("Z", 1, 0, 3), ("ta", 1, 1), ("ot", 1, 0),
-    ("TN", 0, 1, 0), ("th", 0), ("Z", 0, 1, 0), ("Bn", 1, 0), ("Z", 1, 0, 2), ("B", 1, 0), ("TF", 1, 1, 0),
-    ("S", 1, 1, 1), ("TN", 1, 1, 0), ("J", 0, 1, 3), ("W", ("far", 0, 0)), ("S", 1, 1, 0), ("Bn", 1, 1), ("B", 1, 1),
-    ("TF", 1, 1, 1), ("J", 0, 1, 0), ("S", 1, 1, 3), ("Z", 1, 1, 1), ("S", 0, 1, 1), ("S", 1, 1, 2),
-    ("W", ("far", 1, 0)), ("S", 0, 0, 1), ("Z", 1, 1, 0), ("W", ("hop",)), ("TN", 1, 1, 1), ("W", ("near", 0, 1)),
-    ("S", 1, 0, 3), ("J", 1, 1, 1), ("W", ("z", 1)), ("G", 1, 1), ("J", 1, 1, 0), ("C", 0, 1, 0), ("S", 0, 0, 0),
-    ("J", 1, 1, 3), ("Z", 0, 1, 1), ("G", 1, 0), ("C", 0, 1, 2), ("C", 1, 1, 1), ("J", 0, 1, 1), ("C", 0, 1, 3),
-    ("J", 1, 1, 2), ("th", 1), ("S", 1, 0, 0), ("S", 1, 0, 1), ("C", 1, 1, 0), ("C", 1, 1, 3), ("G", 0, 1),
-    ("PO", 0, 2), ("J", 0, 0, 1), ("PO", 0, 0), ("TN", 1, 0, 0), ("W", ("far", 0, 1)), ("J", 1, 0, 3),
-    ("C", 0, 1, 1), ("RL", 2), ("C", 1, 1, 2), ("J", 0, 0, 0), ("PO", 1, 1), ("PO", 0, 3), ("G", 0, 0), ("PO", 1, 3),
-    ("J", 1, 0, 1), ("PO", 1, 0), ("C", 1, 0, 2), ("RL", 3), ("PO", 0, 1), ("J", 1, 0, 0), ("PO", 1, 2),
-    ("GS", 1, 0), ("GS", 0, 1), ("C", 0, 0, 2), ("GS", 1, 1), ("W", ("far", 1, 1)), ("C", 0, 0, 1), ("C", 0, 0, 0),
-    ("C", 1, 0, 3), ("W", ("land",)), ("FIN", 0, 2), ("FIN", 0, 0), ("C", 0, 0, 3), ("FIN", 1, 3), ("C", 1, 0, 1),
-    ("FIN", 1, 1), ("FIN", 0, 3), ("GS", 0, 0), ("FIN", 1, 2), ("C", 1, 0, 0), ("W", ("near", 1, 1)), ("FIN", 1, 0),
-    ("FIN", 0, 1),
-    ("W", ("middle", 0), ("middle", 1), ("term", 0, 0), ("term", 1, 0), ("sum", 0, 0), ("term", 0, 1), ("sum", 1, 0), ("out", 0), ("sum", 0, 1), ("out", 1), ("term", 1, 1), ("sum", 1, 1), ("grad", 1, 1), ("grad", 1, 0), ("grad", 0, 1), ("last",), ("grad", 0, 0)),
+    (S_OZ, 0, 3), (S_OX, 0, 3), (S_OX, 1, 0), (S_OZ, 0, 2), (S_OZ, 0, 1), (S_SU,), (S_OZ, 1, 1), (S_OX, 1, 2),
+    (S_OX, 0, 2), (S_SD,), (S_OX, 0, 1), (S_RX, 0, 0, 3), (S_OX, 0, 0), (S_OZ, 0, 0), (S_RX, 1, 0, 0), (S_OX, 1, 3),
+    (S_RZ, 0, 3), (S_RZ, 0, 2), (S_RX, 1, 0, 2), (S_RZ, 0, 1), (S_OZ, 1, 3), (S_OX, 1, 1), (S_H1, X, NR, 1, 2),
+    (S_RX, 0, 0, 2), (S_FN, 0, 1), (S_RZ, 0, 0), (S_RZ, 1, 1), (S_RX, 0, 0, 1), (S_OZ, 1, 2), (S_H1, Y, FR, 1, 0),
+    (S_TW,), (S_OT, 0, 3), (S_H1, Y, FR, 1, 2), (S_H1, X, FR, 1, 2), (S_RX, 0, 0, 0), (S_F, 0, 1), (S_RZ, 1, 3),
+    (S_OT, 0, 2), (S_RX, 1, 0, 3), (S_H1, X, NR, 1, 0), (S_OT, 0, 1), (S_H1, X, FR, 1, 0), (S_FN, 0, 0),
+    (S_RX, 1, 0, 1), (S_H1, Y, NR, 1, 2), (S_H1, Y, NR, 1, 0), (S_OT, 0, 0), (S_TF, 0, 0, 1), (S_OZ, 1, 0),
+    (S_RX, 0, 1, 3), (S_TN, 0, 0, 1), (S_F, 0, 0), (S_TF, 0, 0, 0), (S_RX, 0, 1, 2), (S_RZ, 1, 2), (S_OT, 1, 1),
+    (S_BN, 0, 1), (S_H2, X, NR, 1, 2), (S_B, 0, 1), (S_TF, 1, 0, 1), (S_RX, 0, 1, 1), (S_TN, 0, 0, 0), (S_OT, 1, 3),
+    (S_S, 0, 0, 2), (S_TN, 1, 0, 1), (S_S, 1, 0, 2), (S_H2, Y, FR, 1, 2), (S_FN, 1, 1), (S_TA, 0, 1), (S_J, 0, 0, 2),
+    (S_RX, 0, 1, 0), (S_F, 1, 1), (S_TF, 0, 1, 1), (S_S, 0, 1, 2), (S_H2, Y, FR, 1, 0), (S_S, 0, 0, 3),
+    (S_RX, 1, 1, 1), (S_H2, X, NR, 1, 0), (S_J, 0, 0, 3), (S_FN, 1, 0), (S_TN, 0, 1, 1), (S_S, 0, 1, 3),
+    (S_RZ, 1, 0), (S_BN, 0, 0), (S_TA, 0, 0), (S_W, 11), (S_H2, X, FR, 1, 0), (S_H2, X, FR, 1, 2), (S_B, 0, 0),
+    (S_H2, Y, NR, 1, 0), (S_W, 25), (S_TF, 1, 0, 0), (S_RX, 1, 1, 3), (S_F, 1, 0), (S_W, 3), (S_J, 1, 0, 2),
+    (S_W, 0), (S_H2, Y, NR, 1, 2), (S_Z, 0, 0, 2), (S_TF, 0, 1, 0), (S_TA, 1, 0), (S_OT, 1, 2), (S_S, 0, 1, 0),
+    (S_Z, 0, 0, 3), (S_J, 0, 1, 2), (S_W, 17), (S_Z, 1, 0, 3), (S_TA, 1, 1), (S_OT, 1, 0), (S_TN, 0, 1, 0),
+    (S_TH, 0), (S_Z, 0, 1, 0), (S_BN, 1, 0), (S_Z, 1, 0, 2), (S_B, 1, 0), (S_TF, 1, 1, 0), (S_S, 1, 1, 1),
+    (S_TN, 1, 1, 0), (S_J, 0, 1, 3), (S_W, 5), (S_S, 1, 1, 0), (S_BN, 1, 1), (S_B, 1, 1), (S_TF, 1, 1, 1),
+    (S_J, 0, 1, 0), (S_S, 1, 1, 3), (S_Z, 1, 1, 1), (S_S, 0, 1, 1), (S_S, 1, 1, 2), (S_W, 19), (S_S, 0, 0, 1),
+    (S_Z, 1, 1, 0), (S_W, 29), (S_TN, 1, 1, 1), (S_W, 4), (S_S, 1, 0, 3), (S_J, 1, 1, 1), (S_W, 14), (S_G, 1, 1),
+    (S_J, 1, 1, 0), (S_C, 0, 1, 0), (S_S, 0, 0, 0), (S_J, 1, 1, 3), (S_Z, 0, 1, 1), (S_G, 1, 0), (S_C, 0, 1, 2),
+    (S_C, 1, 1, 1), (S_J, 0, 1, 1), (S_C, 0, 1, 3), (S_J, 1, 1, 2), (S_TH, 1), (S_S, 1, 0, 0), (S_S, 1, 0, 1),
+    (S_C, 1, 1, 0), (S_C, 1, 1, 3), (S_G, 0, 1), (S_PO, 0, 2), (S_J, 0, 0, 1), (S_PO, 0, 0), (S_TN, 1, 0, 0),
+    (S_W, 6), (S_J, 1, 0, 3), (S_C, 0, 1, 1), (S_RL, 2), (S_C, 1, 1, 2), (S_J, 0, 0, 0), (S_PO, 1, 1), (S_PO, 0, 3),
+    (S_G, 0, 0), (S_PO, 1, 3), (S_J, 1, 0, 1), (S_PO, 1, 0), (S_C, 1, 0, 2), (S_RL, 3), (S_PO, 0, 1), (S_J, 1, 0, 0),
+    (S_PO, 1, 2), (S_GS, 1, 0), (S_GS, 0, 1), (S_C, 0, 0, 2), (S_GS, 1, 1), (S_W, 20), (S_C, 0, 0, 1),
+    (S_C, 0, 0, 0), (S_C, 1, 0, 3), (S_W, 30), (S_FIN, 0, 2), (S_FIN, 0, 0), (S_C, 0, 0, 3), (S_FIN, 1, 3),
+    (S_C, 1, 0, 1), (S_FIN, 1, 1), (S_FIN, 0, 3), (S_GS, 0, 0), (S_FIN, 1, 2), (S_C, 1, 0, 0), (S_W, 18),
+    (S_FIN, 1, 0), (S_FIN, 0, 1), (S_W, 1, 15, 7, 21, 9, 8, 23, 2, 10, 16, 22, 24, 27, 26, 13, 28, 12),
 )
 
 
@@ -133,7 +146,7 @@
             src_ref=src,
             dst_ref=dst,
             send_sem=sends.at[FAMILIES[family(key)]],
-            recv_sem=recvs.at[NUMBER[key]],
+            recv_sem=recvs.at[LANDINGS[arrival(key)]],
             device_id=place[target],
             device_id_type=MESH,
         )
@@ -192,6 +205,17 @@
         slot = int(name == "out3")
         return remote(z_send.at[which, rows(slot, j)], z_recv.at[which, rows(slot, j)], key, "z3" if slot else "z1")
 
+    def together(pieces, sent_by, landed_by):
+        span = held.at[0, 0, pl.ds(0, pieces * PART)]
+        return pltpu.make_async_remote_copy(
+            src_ref=span,
+            dst_ref=span,
+            send_sem=sends.at[sent_by],
+            recv_sem=recvs.at[landed_by],
+            device_id=place["z1"],
+            device_id_type=MESH,
+        )
+
     started, landed, copied, sent = set(), set(), set(), set()
 
     def send(*keys):
@@ -201,32 +225,26 @@
 
     def need(*keys):
         for key in keys:
-            if key not in landed:
-                landed.add(key)
+            name = arrival(key)
+            if name in landed:
+                continue
+            landed.add(name)
+            if name[0] in ("weight", "grad"):
                 transfer(key).wait_recv()
+            else:
+                together(ARRIVALS[name], 0, LANDINGS[name]).wait_recv()
 
     own = [
         pltpu.make_async_copy(shared[which], held.at[which, 0, pl.ds(0, ROWS)], local.at[which])
         for which in range(2)
     ]
     loads = [pltpu.make_async_copy(ref, raw.at[which], local.at[2 + which]) for which, ref in enumerate((up, down))]
-    for copy in loads + own:
-        copy.start()
-
     barrier = pltpu.get_barrier_semaphore()
     for target in place.values():
         pl.semaphore_signal(barrier, inc=1, device_id=target, device_id_type=MESH)
+    for copy in loads + own:
+        copy.start()
     pl.semaphore_wait(barrier, len(place))
-
-    def scale_up(k, carry):
-        factor = mask[0, k].astype(F32)
-        uall[pl.ds(pl.multiple_of(k * G, G), G), pl.ds(0, G)] = (raw[0, k].astype(F32) * factor).astype(BF16)
-        return carry
-
-    def scale_down(k, carry):
-        factor = mask[0, k].astype(F32)
-        dall[pl.ds(0, G), pl.ds(pl.multiple_of(k * G, G), G)] = (raw[1, k].astype(F32) * factor).astype(BF16)
-        return carry
 
     def tile(slot, t):
         return pl.ds(slot * ROWS + t * TILE, TILE)
@@ -261,12 +279,14 @@
 
     def mask_up():
         loads[0].wait()
-        lax.fori_loop(0, LEVELS, scale_up, 0)
+        for k, level in enumerate(LEVEL):
+            uall[pl.ds(k * G, G), pl.ds(0, G)] = (raw[0, level].astype(F32) * mask[0, level].astype(F32)).astype(BF16)
         send(("weight", 0))
 
     def mask_down():
         loads[1].wait()
-        lax.fori_loop(0, LEVELS, scale_down, 0)
+        for k, level in enumerate(LEVEL):
+            dall[pl.ds(0, G), pl.ds(k * G, G)] = (raw[1, level].astype(F32) * mask[0, level].astype(F32)).astype(BF16)
         send(("weight", 1))
 
     def turn_weights():
@@ -306,13 +326,12 @@
                 need(("land", axis, "f", which, j) if slot and (which, j) in MOVED else ("far", axis, which, slot, j))
 
     def partial(which, at, weights):
-        early = jnp.concatenate([held[which, level, at] for level in (0, 1, 2)], axis=1)
-        total = jnp.dot(early, weights[pl.ds(0, 3 * G), :], preferred_element_type=F32)
-        return total + jnp.dot(held[which, 4, at], weights[pl.ds(4 * G, G), :], preferred_element_type=F32)
+        early = jnp.concatenate([held[which, k, at] for k in range(4)], axis=1)
+        return jnp.dot(early, weights[pl.ds(0, 4 * G), :], preferred_element_type=F32)
 
     def rest(which, at, weights):
-        total = jnp.dot(held[which, 3, at], weights[pl.ds(3 * G, G), :], preferred_element_type=F32)
-        return total + jnp.dot(held[which, 5, at], weights[pl.ds(5 * G, G), :], preferred_element_type=F32)
+        late = jnp.concatenate([held[which, k, at] for k in (4, 5)], axis=1)
+        return jnp.dot(late, weights[pl.ds(4 * G, 2 * G), :], preferred_element_type=F32)
 
     def forward_near(slot, t):
         near_inputs(0, slot, t)
@@ -419,45 +438,33 @@
         send(("grad", which, third))
 
     def write_grad(which, k):
-        return pltpu.make_async_copy(grad_own.at[which, k], (gdown if which else gup).at[k], local.at[4 + which * LEVELS + k])
+        return pltpu.make_async_copy(grad_own.at[which, k], (gdown if which else gup).at[LEVEL[k]], local.at[4 + which * LEVELS + k])
 
     def grads_sum(which, third):
         need(("grad", which, third))
 
-        def body(k, carry):
-            grad_own[which, k] = (grad_own[which, k] + grad_recv[which, k]) * mask[0, k].astype(F32)
+        for k in range(third * THIRDS, (third + 1) * THIRDS):
+            total = grad_own[which, k] + grad_recv[which, k]
+            grad_own[which, k] = total * mask[0, LEVEL[k]].astype(F32)
             write_grad(which, k).start()
-            return carry
-
-        lax.fori_loop(third * THIRDS, (third + 1) * THIRDS, body, 0)
-
-    def finish_sends(*names):
-        for name in names:
+
+    def finish_sends(*numbers):
+        for name in (tuple(SIZES)[n] for n in numbers):
             sent.add(name)
             if name[0] in ("weight", "grad"):
                 transfer(name).wait_send()
             else:
-                span = pl.ds(0, SIZES[name] * PART)
-                pltpu.make_async_remote_copy(
-                    src_ref=held.at[0, 0, span],
-                    dst_ref=held.at[0, 0, span],
-                    send_sem=sends.at[FAMILIES[name]],
-                    recv_sem=recvs.at[0],
-                    device_id=place["z1"],
-                    device_id_type=MESH,
-                ).wait_send()
-
-    steps = {
-        "W": finish_sends,
-        "oz": own_z, "ox": own_xy, "rz": relay_z, "ot": other, "rx": relay_xy, "su": mask_up, "sd": mask_down,
-        "tw": turn_weights, "th": turn_held, "ta": turn_act, "F": forward, "B": backward, "h1": hop, "h2": land, "Fn": forward_near, "Bn": backward_near, "TF": far_terms,
-        "TN": near_terms, "S": send_term, "RL": hand_on, "J": join, "C": collect, "Z": plain, "PO": pass_on,
-        "FIN": finish, "G": grads, "GS": grads_sum,
-    }
+                together(SIZES[name], FAMILIES[name], 0).wait_send()
+
+    steps = (
+        own_xy, own_z, relay_z, other, relay_xy, hop, land, mask_up, mask_down, turn_weights, turn_held, turn_act,
+        forward_near, forward, backward_near, backward, far_terms, near_terms, send_term, hand_on, join, collect,
+        plain, pass_on, finish, grads, grads_sum, finish_sends,
+    )
     for step in ORDER:
         steps[step[0]](*step[1:])
 
-    assert started == landed == set(NUMBER)
+    assert started == set(NUMBER) and landed == set(ARRIVALS)
     for which in range(2):
         for k in range(LEVELS):
             write_grad(which, k).wait()
@@ -526,7 +533,7 @@
             pltpu.VMEM((2, LEVELS, G, G), F32),
             pltpu.VMEM((2, LEVELS, G, G), F32),
             pltpu.SemaphoreType.DMA((len(FAMILIES),)),
-            pltpu.SemaphoreType.DMA((COPIES,)),
+            pltpu.SemaphoreType.DMA((len(LANDINGS),)),
             pltpu.SemaphoreType.DMA((4 + 2 * LEVELS,)),
         ],
         compiler_params=pltpu.CompilerParams(

time: 65.1 us -> 63.9 us (0.982)
  Pallas kernels: 64.3 us -> 63.1 us
    pallas_call x1, Pallas kernels: 62.4 us -> 61.2 us  [shards(): pl.pallas_call(kernel, out_shape=tuple((pltpu.VMEM(a.shape, a.dtype) for...]
where the time goes in v4:
time: 63.9 us; the launch traced here: 63.8 us
  Pallas kernels  63.1 us (99%)
  between operations  0.64 us (1%)
    pallas_call x1, Pallas kernels, shards(): pl.pallas_call(kernel, out_shape=tuple((pltpu.VMEM(a.shape, a.dtype) for...  61.2 us
    pallas_call x1, Pallas kernels, shards(): pl.pallas_call(hand_out, out_shape=result, in_specs=[anywhere] * 4, out_s...  1.9 us

profile of v4, /device:TPU:0, one launch (start us, length us, event | category | flops | bytes accessed | tf_op | source)
XLA Modules:
  0.0 63.8 jit_solution(8375959864140669805)
XLA Ops:
  0.6 61.2 %shard_map.84 = (bf16[512,256]{1,0:T(8,128)(2,1)S(1)}, bf16[512,256]{1,0:T(8,128)(2,1)S(1)}, f32[6,256,256]{2,1,0:T(8,128)S(1)}, f32[6,256,256]{2,1,0:T(8,128)S(1)}) custom-call(bf16[512,256]{1,0:T(8,128)(2,1)} %tok.1, bf16[512,256]{1,0:T(8,128)(2,1)} %cot.1, bf16[6,256,256]{2,1,0:T(8,128)(2,1)} %bitcast.4, bf16[6,256,256]{2,1,0:T(8,128)(2,1)} %bitcast.5, ...), custom_call_target="tpu_custom_call" | custom-call | tf_op jit(solution)/shard_map/pallas_call | solution.py:501
  61.9 1.9 %shard_map.85 = (bf16[512,256]{1,0:T(8,128)(2,1)}, bf16[512,256]{1,0:T(8,128)(2,1)}, f32[6,256,256]{2,1,0:T(8,128)}, f32[6,256,256]{2,1,0:T(8,128)}) custom-call(bf16[512,256]{1,0:T(8,128)(2,1)S(1)} %get-tuple-element.12.refs_0_, bf16[512,256]{1,0:T(8,128)(2,1)S(1)} %get-tuple-element.13.refs_1_, f32[6,256,256]{2,1,0:T(8,128)S(1)} %get-tuple-element.14.refs_2_, ...), custom_call_target="tpu_custom_call" | custom-call | tf_op jit(solution)/shard_map/pallas_call | solution.py:544

commit v5 on v4

--- a/solution.py
+++ b/solution.py
@@ -85,35 +85,35 @@
     S_BN, S_B, S_TF, S_TN, S_S, S_RL, S_J, S_C, S_Z, S_PO, S_FIN, S_G, S_GS, S_W = range(28)
 X, Y, NR, FR = "x", "y", "n", "f"
 ORDER = (
-    (S_OZ, 0, 3), (S_OX, 0, 3), (S_OX, 1, 0), (S_OZ, 0, 2), (S_OZ, 0, 1), (S_SU,), (S_OZ, 1, 1), (S_OX, 1, 2),
-    (S_OX, 0, 2), (S_SD,), (S_OX, 0, 1), (S_RX, 0, 0, 3), (S_OX, 0, 0), (S_OZ, 0, 0), (S_RX, 1, 0, 0), (S_OX, 1, 3),
-    (S_RZ, 0, 3), (S_RZ, 0, 2), (S_RX, 1, 0, 2), (S_RZ, 0, 1), (S_OZ, 1, 3), (S_OX, 1, 1), (S_H1, X, NR, 1, 2),
-    (S_RX, 0, 0, 2), (S_FN, 0, 1), (S_RZ, 0, 0), (S_RZ, 1, 1), (S_RX, 0, 0, 1), (S_OZ, 1, 2), (S_H1, Y, FR, 1, 0),
-    (S_TW,), (S_OT, 0, 3), (S_H1, Y, FR, 1, 2), (S_H1, X, FR, 1, 2), (S_RX, 0, 0, 0), (S_F, 0, 1), (S_RZ, 1, 3),
-    (S_OT, 0, 2), (S_RX, 1, 0, 3), (S_H1, X, NR, 1, 0), (S_OT, 0, 1), (S_H1, X, FR, 1, 0), (S_FN, 0, 0),
-    (S_RX, 1, 0, 1), (S_H1, Y, NR, 1, 2), (S_H1, Y, NR, 1, 0), (S_OT, 0, 0), (S_TF, 0, 0, 1), (S_OZ, 1, 0),
-    (S_RX, 0, 1, 3), (S_TN, 0, 0, 1), (S_F, 0, 0), (S_TF, 0, 0, 0), (S_RX, 0, 1, 2), (S_RZ, 1, 2), (S_OT, 1, 1),
-    (S_BN, 0, 1), (S_H2, X, NR, 1, 2), (S_B, 0, 1), (S_TF, 1, 0, 1), (S_RX, 0, 1, 1), (S_TN, 0, 0, 0), (S_OT, 1, 3),
-    (S_S, 0, 0, 2), (S_TN, 1, 0, 1), (S_S, 1, 0, 2), (S_H2, Y, FR, 1, 2), (S_FN, 1, 1), (S_TA, 0, 1), (S_J, 0, 0, 2),
-    (S_RX, 0, 1, 0), (S_F, 1, 1), (S_TF, 0, 1, 1), (S_S, 0, 1, 2), (S_H2, Y, FR, 1, 0), (S_S, 0, 0, 3),
-    (S_RX, 1, 1, 1), (S_H2, X, NR, 1, 0), (S_J, 0, 0, 3), (S_FN, 1, 0), (S_TN, 0, 1, 1), (S_S, 0, 1, 3),
-    (S_RZ, 1, 0), (S_BN, 0, 0), (S_TA, 0, 0), (S_W, 11), (S_H2, X, FR, 1, 0), (S_H2, X, FR, 1, 2), (S_B, 0, 0),
-    (S_H2, Y, NR, 1, 0), (S_W, 25), (S_TF, 1, 0, 0), (S_RX, 1, 1, 3), (S_F, 1, 0), (S_W, 3), (S_J, 1, 0, 2),
-    (S_W, 0), (S_H2, Y, NR, 1, 2), (S_Z, 0, 0, 2), (S_TF, 0, 1, 0), (S_TA, 1, 0), (S_OT, 1, 2), (S_S, 0, 1, 0),
-    (S_Z, 0, 0, 3), (S_J, 0, 1, 2), (S_W, 17), (S_Z, 1, 0, 3), (S_TA, 1, 1), (S_OT, 1, 0), (S_TN, 0, 1, 0),
-    (S_TH, 0), (S_Z, 0, 1, 0), (S_BN, 1, 0), (S_Z, 1, 0, 2), (S_B, 1, 0), (S_TF, 1, 1, 0), (S_S, 1, 1, 1),
-    (S_TN, 1, 1, 0), (S_J, 0, 1, 3), (S_W, 5), (S_S, 1, 1, 0), (S_BN, 1, 1), (S_B, 1, 1), (S_TF, 1, 1, 1),
-    (S_J, 0, 1, 0), (S_S, 1, 1, 3), (S_Z, 1, 1, 1), (S_S, 0, 1, 1), (S_S, 1, 1, 2), (S_W, 19), (S_S, 0, 0, 1),
-    (S_Z, 1, 1, 0), (S_W, 29), (S_TN, 1, 1, 1), (S_W, 4), (S_S, 1, 0, 3), (S_J, 1, 1, 1), (S_W, 14), (S_G, 1, 1),
-    (S_J, 1, 1, 0), (S_C, 0, 1, 0), (S_S, 0, 0, 0), (S_J, 1, 1, 3), (S_Z, 0, 1, 1), (S_G, 1, 0), (S_C, 0, 1, 2),
-    (S_C, 1, 1, 1), (S_J, 0, 1, 1), (S_C, 0, 1, 3), (S_J, 1, 1, 2), (S_TH, 1), (S_S, 1, 0, 0), (S_S, 1, 0, 1),
-    (S_C, 1, 1, 0), (S_C, 1, 1, 3), (S_G, 0, 1), (S_PO, 0, 2), (S_J, 0, 0, 1), (S_PO, 0, 0), (S_TN, 1, 0, 0),
-    (S_W, 6), (S_J, 1, 0, 3), (S_C, 0, 1, 1), (S_RL, 2), (S_C, 1, 1, 2), (S_J, 0, 0, 0), (S_PO, 1, 1), (S_PO, 0, 3),
-    (S_G, 0, 0), (S_PO, 1, 3), (S_J, 1, 0, 1), (S_PO, 1, 0), (S_C, 1, 0, 2), (S_RL, 3), (S_PO, 0, 1), (S_J, 1, 0, 0),
-    (S_PO, 1, 2), (S_GS, 1, 0), (S_GS, 0, 1), (S_C, 0, 0, 2), (S_GS, 1, 1), (S_W, 20), (S_C, 0, 0, 1),
-    (S_C, 0, 0, 0), (S_C, 1, 0, 3), (S_W, 30), (S_FIN, 0, 2), (S_FIN, 0, 0), (S_C, 0, 0, 3), (S_FIN, 1, 3),
-    (S_C, 1, 0, 1), (S_FIN, 1, 1), (S_FIN, 0, 3), (S_GS, 0, 0), (S_FIN, 1, 2), (S_C, 1, 0, 0), (S_W, 18),
-    (S_FIN, 1, 0), (S_FIN, 0, 1), (S_W, 1, 15, 7, 21, 9, 8, 23, 2, 10, 16, 22, 24, 27, 26, 13, 28, 12),
+    (S_OX, 0, 3), (S_OZ, 0, 2), (S_OX, 1, 0), (S_OZ, 0, 3), (S_SU,), (S_SD,), (S_OX, 1, 2), (S_OZ, 0, 0),
+    (S_RX, 0, 0, 3), (S_OX, 0, 2), (S_OZ, 0, 1), (S_OX, 0, 1), (S_RX, 1, 0, 0), (S_OX, 0, 0), (S_RZ, 0, 3),
+    (S_OZ, 1, 1), (S_OX, 1, 3), (S_RZ, 0, 2), (S_OZ, 1, 3), (S_RX, 1, 0, 2), (S_H1, Y, NR, 1, 2), (S_RZ, 0, 0),
+    (S_OX, 1, 1), (S_RX, 0, 0, 2), (S_RZ, 0, 1), (S_OZ, 1, 2), (S_H1, X, NR, 1, 0), (S_FN, 0, 1),
+    (S_H1, Y, FR, 1, 0), (S_RX, 0, 0, 1), (S_OT, 0, 3), (S_TW,), (S_RX, 0, 0, 0), (S_FN, 0, 0), (S_RX, 1, 0, 3),
+    (S_OT, 0, 2), (S_F, 0, 1), (S_RZ, 1, 1), (S_OT, 0, 0), (S_RZ, 1, 3), (S_RX, 1, 0, 1), (S_TF, 0, 0, 1),
+    (S_TN, 0, 0, 1), (S_H1, X, FR, 1, 0), (S_OT, 0, 1), (S_H1, X, FR, 1, 2), (S_J, 0, 0, 2), (S_RX, 0, 1, 3),
+    (S_OZ, 1, 0), (S_H1, Y, FR, 1, 2), (S_J, 0, 0, 3), (S_F, 0, 0), (S_RX, 0, 1, 2), (S_FN, 1, 1), (S_TF, 0, 0, 0),
+    (S_BN, 0, 1), (S_RZ, 1, 2), (S_H1, Y, NR, 1, 0), (S_RX, 0, 1, 0), (S_B, 0, 1), (S_TF, 1, 0, 1), (S_TN, 0, 0, 0),
+    (S_OT, 1, 1), (S_RX, 0, 1, 1), (S_H1, X, NR, 1, 2), (S_S, 0, 0, 2), (S_H2, Y, FR, 1, 0), (S_FN, 1, 0),
+    (S_S, 1, 0, 2), (S_H2, X, FR, 1, 0), (S_OT, 1, 3), (S_F, 1, 1), (S_TF, 0, 1, 1), (S_S, 0, 1, 3), (S_TA, 0, 0),
+    (S_H2, X, NR, 1, 0), (S_TN, 1, 0, 1), (S_BN, 0, 0), (S_B, 0, 0), (S_RZ, 1, 0), (S_S, 0, 1, 2), (S_F, 1, 0),
+    (S_OT, 1, 2), (S_TF, 0, 1, 0), (S_W, 11), (S_H2, Y, NR, 1, 0), (S_W, 25), (S_TA, 0, 1), (S_H2, Y, FR, 1, 2),
+    (S_TN, 0, 1, 0), (S_TN, 0, 1, 1), (S_RX, 1, 1, 1), (S_W, 0), (S_H2, X, FR, 1, 2), (S_S, 0, 1, 0),
+    (S_H2, X, NR, 1, 2), (S_W, 3), (S_J, 0, 1, 3), (S_J, 1, 0, 2), (S_Z, 0, 0, 3), (S_H2, Y, NR, 1, 2),
+    (S_S, 0, 0, 3), (S_TH, 1), (S_TF, 1, 0, 0), (S_TA, 1, 0), (S_J, 0, 1, 2), (S_W, 17), (S_OT, 1, 0),
+    (S_RX, 1, 1, 3), (S_Z, 1, 0, 3), (S_Z, 0, 1, 1), (S_BN, 1, 0), (S_B, 1, 0), (S_TF, 1, 1, 0), (S_S, 1, 1, 1),
+    (S_S, 1, 1, 0), (S_TN, 1, 1, 0), (S_W, 5), (S_C, 0, 1, 3), (S_Z, 1, 1, 1), (S_J, 0, 1, 0), (S_TA, 1, 1),
+    (S_Z, 1, 0, 2), (S_S, 0, 1, 1), (S_Z, 0, 1, 0), (S_Z, 0, 0, 2), (S_W, 19), (S_Z, 1, 1, 0), (S_BN, 1, 1),
+    (S_B, 1, 1), (S_G, 1, 1), (S_W, 4), (S_J, 1, 1, 1), (S_TF, 1, 1, 1), (S_S, 1, 1, 3), (S_S, 1, 1, 2), (S_W, 14),
+    (S_S, 0, 0, 1), (S_S, 0, 0, 0), (S_S, 1, 0, 3), (S_J, 1, 1, 0), (S_TN, 1, 1, 1), (S_C, 0, 1, 2), (S_S, 1, 0, 0),
+    (S_C, 0, 1, 0), (S_J, 0, 1, 1), (S_G, 1, 0), (S_C, 1, 1, 1), (S_J, 1, 1, 3), (S_TH, 0), (S_J, 1, 1, 2),
+    (S_C, 1, 1, 0), (S_W, 6), (S_PO, 0, 0), (S_W, 29), (S_G, 0, 1), (S_J, 0, 0, 1), (S_C, 0, 1, 1), (S_C, 1, 1, 3),
+    (S_PO, 0, 2), (S_S, 1, 0, 1), (S_J, 0, 0, 0), (S_PO, 0, 3), (S_TN, 1, 0, 0), (S_C, 1, 1, 2), (S_C, 0, 0, 2),
+    (S_PO, 1, 1), (S_J, 1, 0, 3), (S_G, 0, 0), (S_RL, 3), (S_J, 1, 0, 0), (S_PO, 1, 3), (S_PO, 1, 0), (S_C, 0, 0, 3),
+    (S_RL, 2), (S_J, 1, 0, 1), (S_C, 1, 0, 2), (S_PO, 0, 1), (S_GS, 0, 1), (S_PO, 1, 2), (S_GS, 1, 1), (S_GS, 1, 0),
+    (S_C, 1, 0, 3), (S_FIN, 1, 3), (S_C, 1, 0, 0), (S_FIN, 1, 0), (S_FIN, 0, 3), (S_W, 30), (S_C, 0, 0, 1),
+    (S_C, 0, 0, 0), (S_FIN, 0, 0), (S_GS, 0, 0), (S_FIN, 0, 2), (S_C, 1, 0, 1), (S_W, 18), (S_FIN, 1, 1), (S_W, 20),
+    (S_FIN, 1, 2), (S_FIN, 0, 1), (S_W, 1, 15, 9, 7, 21, 8, 10, 23, 2, 16, 22, 27, 24, 26, 13, 12, 28),
 )
 
 

time: 63.9 us -> 64.2 us (level)
  no operation moved by 1% of the time
where the time goes in v5:
time: 64.2 us; the launch traced here: 64 us
  Pallas kernels  63.4 us (99%)
    pallas_call x1, Pallas kernels, shards(): pl.pallas_call(kernel, out_shape=tuple((pltpu.VMEM(a.shape, a.dtype) for...  61.5 us
    pallas_call x1, Pallas kernels, shards(): pl.pallas_call(hand_out, out_shape=result, in_specs=[anywhere] * 4, out_s...  1.9 us

profile of v5, /device:TPU:0, one launch (start us, length us, event | category | flops | bytes accessed | tf_op | source)
XLA Modules:
  0.0 64.0 jit_solution(11250049563108755524)
XLA Ops:
  0.6 61.5 %shard_map.84 = (bf16[512,256]{1,0:T(8,128)(2,1)S(1)}, bf16[512,256]{1,0:T(8,128)(2,1)S(1)}, f32[6,256,256]{2,1,0:T(8,128)S(1)}, f32[6,256,256]{2,1,0:T(8,128)S(1)}) custom-call(bf16[512,256]{1,0:T(8,128)(2,1)} %tok.1, bf16[512,256]{1,0:T(8,128)(2,1)} %cot.1, bf16[6,256,256]{2,1,0:T(8,128)(2,1)} %bitcast.4, bf16[6,256,256]{2,1,0:T(8,128)(2,1)} %bitcast.5, ...), custom_call_target="tpu_custom_call" | custom-call | tf_op jit(solution)/shard_map/pallas_call | solution.py:501
  62.1 1.9 %shard_map.85 = (bf16[512,256]{1,0:T(8,128)(2,1)}, bf16[512,256]{1,0:T(8,128)(2,1)}, f32[6,256,256]{2,1,0:T(8,128)}, f32[6,256,256]{2,1,0:T(8,128)}) custom-call(bf16[512,256]{1,0:T(8,128)(2,1)S(1)} %get-tuple-element.12.refs_0_, bf16[512,256]{1,0:T(8,128)(2,1)S(1)} %get-tuple-element.13.refs_1_, f32[6,256,256]{2,1,0:T(8,128)S(1)} %get-tuple-element.14.refs_2_, ...), custom_call_target="tpu_custom_call" | custom-call | tf_op jit(solution)/shard_map/pallas_call | solution.py:544

commit v6 on v4

--- a/solution.py
+++ b/solution.py
@@ -122,8 +122,8 @@
 
 
 def kernel(
-    tok, cot, up, down, mask, out, gtok, gup, gdown,
-    held, held_t, raw, uall, dall, uall_t, dall_t, act, act_t, gpre, slope, gact,
+    tok, cot, up, down, present, out, gtok, gup, gdown,
+    mask, held, held_t, raw, uall, dall, uall_t, dall_t, act, act_t, gpre, slope, gact,
     term_send, term_recv, near_term, sum_send, sum_recv, base, z_term,
     half_send, half_recv, last_recv, hops, z_send, z_recv,
     grad_own, grad_peer, grad_recv,
@@ -239,9 +239,11 @@
         for which in range(2)
     ]
     loads = [pltpu.make_async_copy(ref, raw.at[which], local.at[2 + which]) for which, ref in enumerate((up, down))]
+    mask_load = pltpu.make_async_copy(present, mask, local.at[4 + 2 * LEVELS])
     barrier = pltpu.get_barrier_semaphore()
     for target in place.values():
         pl.semaphore_signal(barrier, inc=1, device_id=target, device_id_type=MESH)
+    mask_load.start()
     for copy in loads + own:
         copy.start()
     pl.semaphore_wait(barrier, len(place))
@@ -277,13 +279,20 @@
         need(("hop", axis, level, which, j))
         send(("land", axis, level, which, j))
 
+    def mask_loaded():
+        if "mask" not in copied:
+            copied.add("mask")
+            mask_load.wait()
+
     def mask_up():
+        mask_loaded()
         loads[0].wait()
         for k, level in enumerate(LEVEL):
             uall[pl.ds(k * G, G), pl.ds(0, G)] = (raw[0, level].astype(F32) * mask[0, level].astype(F32)).astype(BF16)
         send(("weight", 0))
 
     def mask_down():
+        mask_loaded()
         loads[1].wait()
         for k, level in enumerate(LEVEL):
             dall[pl.ds(0, G), pl.ds(k * G, G)] = (raw[1, level].astype(F32) * mask[0, level].astype(F32)).astype(BF16)
@@ -497,13 +506,14 @@
         jax.ShapeDtypeStruct((LEVELS, G, G), F32),
         jax.ShapeDtypeStruct((LEVELS, G, G), F32),
     )
-    operands = [pltpu.with_memory_space_constraint(a, pltpu.HBM) for a in (tokens, cotangent, up_weight[0], down_weight[0])]
+    operands = [pltpu.with_memory_space_constraint(a, pltpu.HBM) for a in (tokens, cotangent, up_weight[0], down_weight[0], block_mask)]
     worked = pl.pallas_call(
         kernel,
         out_shape=tuple(pltpu.VMEM(a.shape, a.dtype) for a in result),
-        in_specs=[anywhere, anywhere, anywhere, anywhere, pl.BlockSpec(memory_space=pltpu.SMEM)],
+        in_specs=[anywhere] * 5,
         out_specs=(vmem, vmem, anywhere, anywhere),
         scratch_shapes=[
+            pltpu.SMEM((1, LEVELS), jnp.int32),
             pltpu.VMEM((2, LEVELS, both, G), BF16),
             pltpu.VMEM((WIDE, both), BF16),
             pltpu.VMEM((2, LEVELS, G, G), BF16),
@@ -534,12 +544,12 @@
             pltpu.VMEM((2, LEVELS, G, G), F32),
             pltpu.SemaphoreType.DMA((len(FAMILIES),)),
             pltpu.SemaphoreType.DMA((len(LANDINGS),)),
-            pltpu.SemaphoreType.DMA((4 + 2 * LEVELS,)),
+            pltpu.SemaphoreType.DMA((5 + 2 * LEVELS,)),
         ],
         compiler_params=pltpu.CompilerParams(
             collective_id=0, has_side_effects=True, vmem_limit_bytes=58 * 1024 * 1024
         ),
-    )(*operands, block_mask)
+    )(*operands)
     worked = [pltpu.with_memory_space_constraint(a, pltpu.VMEM) for a in worked]
     output, grad_tokens, grad_up, grad_down = pl.pallas_call(
         hand_out,

time: 63.9 us -> 63.2 us (0.989)
    pallas_call x1, Pallas kernels: 61.2 us -> 60.6 us  [shards(): pl.pallas_call(kernel, out_shape=tuple((pltpu.VMEM(a.shape, a.dtype) for...]
where the time goes in v6:
time: 63.2 us; the launch traced here: 63.1 us
  Pallas kernels  62.5 us (99%)
  between operations  0.64 us (1%)
    pallas_call x1, Pallas kernels, shards(): pl.pallas_call(kernel, out_shape=tuple((pltpu.VMEM(a.shape, a.dtype) for...  60.6 us
    pallas_call x1, Pallas kernels, shards(): pl.pallas_call(hand_out, out_shape=result, in_specs=[anywhere] * 4, out_s...  1.9 us

profile of v6, /device:TPU:0, one launch (start us, length us, event | category | flops | bytes accessed | tf_op | source)
XLA Modules:
  0.0 63.1 jit_solution(15721398602488069939)
XLA Ops:
  0.6 60.6 %shard_map.84 = (bf16[512,256]{1,0:T(8,128)(2,1)S(1)}, bf16[512,256]{1,0:T(8,128)(2,1)S(1)}, f32[6,256,256]{2,1,0:T(8,128)S(1)}, f32[6,256,256]{2,1,0:T(8,128)S(1)}) custom-call(bf16[512,256]{1,0:T(8,128)(2,1)} %tok.1, bf16[512,256]{1,0:T(8,128)(2,1)} %cot.1, bf16[6,256,256]{2,1,0:T(8,128)(2,1)} %bitcast.4, bf16[6,256,256]{2,1,0:T(8,128)(2,1)} %bitcast.5, ...), custom_call_target="tpu_custom_call" | custom-call | tf_op jit(solution)/shard_map/pallas_call | solution.py:510
  61.2 1.9 %shard_map.85 = (bf16[512,256]{1,0:T(8,128)(2,1)}, bf16[512,256]{1,0:T(8,128)(2,1)}, f32[6,256,256]{2,1,0:T(8,128)}, f32[6,256,256]{2,1,0:T(8,128)}) custom-call(bf16[512,256]{1,0:T(8,128)(2,1)S(1)} %get-tuple-element.12.refs_0_, bf16[512,256]{1,0:T(8,128)(2,1)S(1)} %get-tuple-element.13.refs_1_, f32[6,256,256]{2,1,0:T(8,128)S(1)} %get-tuple-element.14.refs_2_, ...), custom_call_target="tpu_custom_call" | custom-call | tf_op jit(solution)/shard_map/pallas_call | solution.py:554

commit v7 on v6

--- a/solution.py
+++ b/solution.py
@@ -125,7 +125,7 @@
     tok, cot, up, down, present, out, gtok, gup, gdown,
     mask, held, held_t, raw, uall, dall, uall_t, dall_t, act, act_t, gpre, slope, gact,
     term_send, term_recv, near_term, sum_send, sum_recv, base, z_term,
-    half_send, half_recv, last_recv, hops, z_send, z_recv,
+    half_send, half_recv, last_recv, hops, z_send, z_recv, final,
     grad_own, grad_peer, grad_recv,
     sends, recvs, local,
 ):
@@ -428,7 +428,12 @@
         if passed(which, 0, j):
             need(("last", "x", j), ("last", "y", j))
             total = total + last_recv[0, piece(j)].astype(F32) + last_recv[1, piece(j)].astype(F32)
-        (gtok if which else out)[piece(j), :] = total.astype(BF16)
+        final[which, piece(j)] = total.astype(BF16)
+        write_final(which, j).start()
+
+    def write_final(which, j):
+        number = 5 + 2 * LEVELS + which * PIECES + j
+        return pltpu.make_async_copy(final.at[which, piece(j)], (gtok if which else out).at[piece(j)], local.at[number])
 
     def grads(which, third):
         def body(k, carry):
@@ -477,6 +482,8 @@
     for which in range(2):
         for k in range(LEVELS):
             write_grad(which, k).wait()
+        for j in range(PIECES):
+            write_final(which, j).wait()
     assert sent == set(FAMILIES)
 
 
@@ -498,7 +505,6 @@
 
 def shards(tokens, up_weight, down_weight, block_mask, cotangent):
     anywhere = pl.BlockSpec(memory_space=pl.ANY)
-    vmem = pl.BlockSpec(memory_space=pltpu.VMEM)
     both = 2 * ROWS
     result = (
         jax.ShapeDtypeStruct((ROWS, G), BF16),
@@ -511,7 +517,7 @@
         kernel,
         out_shape=tuple(pltpu.VMEM(a.shape, a.dtype) for a in result),
         in_specs=[anywhere] * 5,
-        out_specs=(vmem, vmem, anywhere, anywhere),
+        out_specs=[anywhere] * 4,
         scratch_shapes=[
             pltpu.SMEM((1, LEVELS), jnp.int32),
             pltpu.VMEM((2, LEVELS, both, G), BF16),
@@ -539,12 +545,13 @@
             pltpu.VMEM((2, 2, len(MOVED) * PART, G), BF16),
             pltpu.VMEM((2, both, G), BF16),
             pltpu.VMEM((2, both, G), BF16),
+            pltpu.VMEM((2, ROWS, G), BF16),
             pltpu.VMEM((2, LEVELS, G, G), F32),
             pltpu.VMEM((2, LEVELS, G, G), F32),
             pltpu.VMEM((2, LEVELS, G, G), F32),
             pltpu.SemaphoreType.DMA((len(FAMILIES),)),
             pltpu.SemaphoreType.DMA((len(LANDINGS),)),
-            pltpu.SemaphoreType.DMA((5 + 2 * LEVELS,)),
+            pltpu.SemaphoreType.DMA((5 + 2 * LEVELS + 2 * PIECES,)),
         ],
         compiler_params=pltpu.CompilerParams(
             collective_id=0, has_side_effects=True, vmem_limit_bytes=58 * 1024 * 1024

time: 63.2 us -> 63.6 us (level)
  no operation moved by 1% of the time
where the time goes in v7:
time: 63.6 us; the launch traced here: 63.5 us
  Pallas kernels  62.8 us (99%)
  between operations  0.64 us (1%)
    pallas_call x1, Pallas kernels, shards(): pl.pallas_call(kernel, out_shape=tuple((pltpu.VMEM(a.shape, a.dtype) for...  60.9 us
    pallas_call x1, Pallas kernels, shards(): pl.pallas_call(hand_out, out_shape=result, in_specs=[anywhere] * 4, out_s...  1.9 us

profile of v7, /device:TPU:0, one launch (start us, length us, event | category | flops | bytes accessed | tf_op | source)
XLA Modules:
  0.0 63.5 jit_solution(14933307588811212661)
XLA Ops:
  0.6 60.9 %shard_map.84 = (bf16[512,256]{1,0:T(8,128)(2,1)S(1)}, bf16[512,256]{1,0:T(8,128)(2,1)S(1)}, f32[6,256,256]{2,1,0:T(8,128)S(1)}, f32[6,256,256]{2,1,0:T(8,128)S(1)}) custom-call(bf16[512,256]{1,0:T(8,128)(2,1)} %tok.1, bf16[512,256]{1,0:T(8,128)(2,1)} %cot.1, bf16[6,256,256]{2,1,0:T(8,128)(2,1)} %bitcast.4, bf16[6,256,256]{2,1,0:T(8,128)(2,1)} %bitcast.5, ...), custom_call_target="tpu_custom_call" | custom-call | tf_op jit(solution)/shard_map/pallas_call | solution.py:516
  61.6 1.9 %shard_map.85 = (bf16[512,256]{1,0:T(8,128)(2,1)}, bf16[512,256]{1,0:T(8,128)(2,1)}, f32[6,256,256]{2,1,0:T(8,128)}, f32[6,256,256]{2,1,0:T(8,128)}) custom-call(bf16[512,256]{1,0:T(8,128)(2,1)S(1)} %get-tuple-element.12.refs_0_, bf16[512,256]{1,0:T(8,128)(2,1)S(1)} %get-tuple-element.13.refs_1_, f32[6,256,256]{2,1,0:T(8,128)S(1)} %get-tuple-element.14.refs_2_, ...), custom_call_target="tpu_custom_call" | custom-call | tf_op jit(solution)/shard_map/pallas_call | solution.py:561

commit v8 on v6

--- a/solution.py
+++ b/solution.py
@@ -131,6 +131,7 @@
 ):
     shared = (tok, cot)
     seq, tp = lax.axis_index("seq"), lax.axis_index("tp")
+    core = lax.rem(seq, 2)
     place = {
         "core": (flip(seq, 1), tp),
         "z1": (seq, flip(tp, 1)),
@@ -279,24 +280,22 @@
         need(("hop", axis, level, which, j))
         send(("land", axis, level, which, j))
 
-    def mask_loaded():
-        if "mask" not in copied:
-            copied.add("mask")
+    def mask_up(late=True):
+        @pl.when(core == (0 if late else 1))
+        def _():
             mask_load.wait()
-
-    def mask_up():
-        mask_loaded()
-        loads[0].wait()
-        for k, level in enumerate(LEVEL):
-            uall[pl.ds(k * G, G), pl.ds(0, G)] = (raw[0, level].astype(F32) * mask[0, level].astype(F32)).astype(BF16)
-        send(("weight", 0))
-
-    def mask_down():
-        mask_loaded()
-        loads[1].wait()
-        for k, level in enumerate(LEVEL):
-            dall[pl.ds(0, G), pl.ds(k * G, G)] = (raw[1, level].astype(F32) * mask[0, level].astype(F32)).astype(BF16)
-        send(("weight", 1))
+            loads[0].wait()
+            for k, level in enumerate(LEVEL):
+                uall[pl.ds(k * G, G), pl.ds(0, G)] = (raw[0, level].astype(F32) * mask[0, level].astype(F32)).astype(BF16)
+            send(("weight", 0))
+
+    def mask_down(late=True):
+        @pl.when(core == (0 if late else 1))
+        def _():
+            loads[1].wait()
+            for k, level in enumerate(LEVEL):
+                dall[pl.ds(0, G), pl.ds(k * G, G)] = (raw[1, level].astype(F32) * mask[0, level].astype(F32)).astype(BF16)
+            send(("weight", 1))
 
     def turn_weights():
         need(("weight", 0), ("weight", 1))
@@ -470,6 +469,8 @@
         forward_near, forward, backward_near, backward, far_terms, near_terms, send_term, hand_on, join, collect,
         plain, pass_on, finish, grads, grads_sum, finish_sends,
     )
+    mask_up(late=False)
+    mask_down(late=False)
     for step in ORDER:
         steps[step[0]](*step[1:])
 

time: 63.2 us -> 63.5 us (level)
  no operation moved by 1% of the time
where the time goes in v8:
time: 63.5 us; the launch traced here: 63.4 us
  Pallas kernels  62.7 us (99%)
  between operations  0.64 us (1%)
    pallas_call x1, Pallas kernels, shards(): pl.pallas_call(kernel, out_shape=tuple((pltpu.VMEM(a.shape, a.dtype) for...  60.8 us
    pallas_call x1, Pallas kernels, shards(): pl.pallas_call(hand_out, out_shape=result, in_specs=[anywhere] * 4, out_s...  1.9 us

profile of v8, /device:TPU:0, one launch (start us, length us, event | category | flops | bytes accessed | tf_op | source)
XLA Modules:
  0.0 63.4 jit_solution(13149727666072378237)
XLA Ops:
  0.6 60.8 %shard_map.84 = (bf16[512,256]{1,0:T(8,128)(2,1)S(1)}, bf16[512,256]{1,0:T(8,128)(2,1)S(1)}, f32[6,256,256]{2,1,0:T(8,128)S(1)}, f32[6,256,256]{2,1,0:T(8,128)S(1)}) custom-call(bf16[512,256]{1,0:T(8,128)(2,1)} %tok.1, bf16[512,256]{1,0:T(8,128)(2,1)} %cot.1, bf16[6,256,256]{2,1,0:T(8,128)(2,1)} %bitcast.4, bf16[6,256,256]{2,1,0:T(8,128)(2,1)} %bitcast.5, ...), custom_call_target="tpu_custom_call" | custom-call | tf_op jit(solution)/shard_map/pallas_call | solution.py:511
  61.5 1.9 %shard_map.85 = (bf16[512,256]{1,0:T(8,128)(2,1)}, bf16[512,256]{1,0:T(8,128)(2,1)}, f32[6,256,256]{2,1,0:T(8,128)}, f32[6,256,256]{2,1,0:T(8,128)}) custom-call(bf16[512,256]{1,0:T(8,128)(2,1)S(1)} %get-tuple-element.12.refs_0_, bf16[512,256]{1,0:T(8,128)(2,1)S(1)} %get-tuple-element.13.refs_1_, f32[6,256,256]{2,1,0:T(8,128)S(1)} %get-tuple-element.14.refs_2_, ...), custom_call_target="tpu_custom_call" | custom-call | tf_op jit(solution)/shard_map/pallas_call | solution.py:555

commit v9 on v6

--- a/solution.py
+++ b/solution.py
@@ -121,9 +121,13 @@
     return index + bit - 2 * bit * lax.rem(lax.div(index, bit), 2)
 
 
+def dot_nt(a, b):
+    return lax.dot_general(a, b, (((1,), (1,)), ((), ())), preferred_element_type=F32)
+
+
 def kernel(
     tok, cot, up, down, present, out, gtok, gup, gdown,
-    mask, held, held_t, raw, uall, dall, uall_t, dall_t, act, act_t, gpre, slope, gact,
+    mask, held, held_t, raw, uall, dall, act, act_t, gpre, slope, gact,
     term_send, term_recv, near_term, sum_send, sum_recv, base, z_term,
     half_send, half_recv, last_recv, hops, z_send, z_recv,
     grad_own, grad_peer, grad_recv,
@@ -301,14 +305,6 @@
     def turn_weights():
         need(("weight", 0), ("weight", 1))
 
-        def body(k, carry):
-            at = pl.ds(pl.multiple_of(k * G, G), G)
-            dall_t[at, :] = dall[:, at].T
-            uall_t[:, at] = uall[at, :].T
-            return carry
-
-        lax.fori_loop(0, LEVELS, body, 0)
-
     def turn_held(slot):
         def body(k, carry):
             at = pl.ds(pl.multiple_of(k * G, G), G)
@@ -334,27 +330,26 @@
             for axis in "xy":
                 need(("land", axis, "f", which, j) if slot and (which, j) in MOVED else ("far", axis, which, slot, j))
 
-    def partial(which, at, weights):
-        early = jnp.concatenate([held[which, k, at] for k in range(4)], axis=1)
-        return jnp.dot(early, weights[pl.ds(0, 4 * G), :], preferred_element_type=F32)
-
-    def rest(which, at, weights):
-        late = jnp.concatenate([held[which, k, at] for k in (4, 5)], axis=1)
-        return jnp.dot(late, weights[pl.ds(4 * G, 2 * G), :], preferred_element_type=F32)
+    def share(which, at, places):
+        inputs = jnp.concatenate([held[which, k, at] for k in places], axis=1)
+        span = pl.ds(places[0] * G, len(places) * G)
+        if which:
+            return dot_nt(inputs, dall[:, span])
+        return jnp.dot(inputs, uall[span, :], preferred_element_type=F32)
 
     def forward_near(slot, t):
         near_inputs(0, slot, t)
         need(("weight", 0))
-        slope[tile(slot, t), :] = partial(0, tile(slot, t), uall)
+        slope[tile(slot, t), :] = share(0, tile(slot, t), (0, 1, 2, 3))
 
     def backward_near(slot, t):
         near_inputs(1, slot, t)
-        gact[tile(slot, t), :] = partial(1, tile(slot, t), dall_t)
+        gact[tile(slot, t), :] = share(1, tile(slot, t), (0, 1, 2, 3))
 
     def forward(slot, t):
         far_inputs(0, slot, t)
         at = tile(slot, t)
-        pre = slope[at, :] + rest(0, at, uall)
+        pre = slope[at, :] + share(0, at, (4, 5))
         square = pre * pre
         tanh = jnp.tanh(SCALE * pre * (1.0 + CUBE * square))
         cdf = 0.5 + 0.5 * tanh
@@ -364,11 +359,11 @@
     def backward(slot, t):
         far_inputs(1, slot, t)
         at = tile(slot, t)
-        gpre[at, :] = ((gact[at, :] + rest(1, at, dall_t)) * slope[at, :]).astype(BF16)
+        gpre[at, :] = ((gact[at, :] + share(1, at, (4, 5))) * slope[at, :]).astype(BF16)
 
     def product(which, slot, t, level):
         if which:
-            return jnp.dot(gpre[tile(slot, t), :], uall_t[:, columns(level)], preferred_element_type=F32)
+            return dot_nt(gpre[tile(slot, t), :], uall[columns(level), :])
         return jnp.dot(act[tile(slot, t), :], dall[:, columns(level)], preferred_element_type=F32)
 
     def far_terms(which, slot, t):
@@ -519,8 +514,6 @@
             pltpu.VMEM((2, LEVELS, G, G), BF16),
             pltpu.VMEM((WIDE, 2 * G), BF16),
             pltpu.VMEM((2 * G, WIDE), BF16),
-            pltpu.VMEM((2 * G, WIDE), BF16),
-            pltpu.VMEM((WIDE, 2 * G), BF16),
             pltpu.VMEM((both, 2 * G), BF16),
             pltpu.VMEM((2 * G, both), BF16),
             pltpu.VMEM((both, 2 * G), BF16),

time: 63.2 us -> 63.6 us (level)
  no operation moved by 1% of the time
where the time goes in v9:
time: 63.6 us; the launch traced here: 63.5 us
  Pallas kernels  62.8 us (99%)
  between operations  0.64 us (1%)
    pallas_call x1, Pallas kernels, shards(): pl.pallas_call(kernel, out_shape=tuple((pltpu.VMEM(a.shape, a.dtype) for...  60.9 us
    pallas_call x1, Pallas kernels, shards(): pl.pallas_call(hand_out, out_shape=result, in_specs=[anywhere] * 4, out_s...  1.9 us

profile of v9, /device:TPU:0, one launch (start us, length us, event | category | flops | bytes accessed | tf_op | source)
XLA Modules:
  0.0 63.5 jit_solution(13187261140533334791)
XLA Ops:
  0.6 60.9 %shard_map.84 = (bf16[512,256]{1,0:T(8,128)(2,1)S(1)}, bf16[512,256]{1,0:T(8,128)(2,1)S(1)}, f32[6,256,256]{2,1,0:T(8,128)S(1)}, f32[6,256,256]{2,1,0:T(8,128)S(1)}) custom-call(bf16[512,256]{1,0:T(8,128)(2,1)} %tok.1, bf16[512,256]{1,0:T(8,128)(2,1)} %cot.1, bf16[6,256,256]{2,1,0:T(8,128)(2,1)} %bitcast.4, bf16[6,256,256]{2,1,0:T(8,128)(2,1)} %bitcast.5, ...), custom_call_target="tpu_custom_call" | custom-call | tf_op jit(solution)/shard_map/pallas_call | solution.py:505
  61.6 1.9 %shard_map.85 = (bf16[512,256]{1,0:T(8,128)(2,1)}, bf16[512,256]{1,0:T(8,128)(2,1)}, f32[6,256,256]{2,1,0:T(8,128)}, f32[6,256,256]{2,1,0:T(8,128)}) custom-call(bf16[512,256]{1,0:T(8,128)(2,1)S(1)} %get-tuple-element.12.refs_0_, bf16[512,256]{1,0:T(8,128)(2,1)S(1)} %get-tuple-element.13.refs_1_, f32[6,256,256]{2,1,0:T(8,128)S(1)} %get-tuple-element.14.refs_2_, ...), custom_call_target="tpu_custom_call" | custom-call | tf_op jit(solution)/shard_map/pallas_call | solution.py:547

commit v10 on v6

--- a/solution.py
+++ b/solution.py
@@ -436,11 +436,11 @@
             if which:
                 both = jnp.dot(act_t[...], held[1, k], preferred_element_type=F32)
                 grad_own[1, k] = both[:G]
-                grad_peer[1, k] = both[G:]
+                grad_peer[1, k] = both[G:].astype(BF16)
             else:
                 both = jnp.dot(held_t[at, :], gpre[...], preferred_element_type=F32)
                 grad_own[0, k] = both[:, :G]
-                grad_peer[0, k] = both[:, G:]
+                grad_peer[0, k] = both[:, G:].astype(BF16)
             return carry
 
         lax.fori_loop(third * THIRDS, (third + 1) * THIRDS, body, 0)
@@ -453,7 +453,7 @@
         need(("grad", which, third))
 
         for k in range(third * THIRDS, (third + 1) * THIRDS):
-            total = grad_own[which, k] + grad_recv[which, k]
+            total = grad_own[which, k] + grad_recv[which, k].astype(F32)
             grad_own[which, k] = total * mask[0, LEVEL[k]].astype(F32)
             write_grad(which, k).start()
 
@@ -540,8 +540,8 @@
             pltpu.VMEM((2, both, G), BF16),
             pltpu.VMEM((2, both, G), BF16),
             pltpu.VMEM((2, LEVELS, G, G), F32),
-            pltpu.VMEM((2, LEVELS, G, G), F32),
-            pltpu.VMEM((2, LEVELS, G, G), F32),
+            pltpu.VMEM((2, LEVELS, G, G), BF16),
+            pltpu.VMEM((2, LEVELS, G, G), BF16),
             pltpu.SemaphoreType.DMA((len(FAMILIES),)),
             pltpu.SemaphoreType.DMA((len(LANDINGS),)),
             pltpu.SemaphoreType.DMA((5 + 2 * LEVELS,)),

time: 63.2 us -> 63.2 us (level)
  no operation moved by 1% of the time
where the time goes in v10:
time: 63.2 us; the launch traced here: 63.1 us
  Pallas kernels  62.5 us (99%)
  between operations  0.64 us (1%)
    pallas_call x1, Pallas kernels, shards(): pl.pallas_call(kernel, out_shape=tuple((pltpu.VMEM(a.shape, a.dtype) for...  60.6 us
    pallas_call x1, Pallas kernels, shards(): pl.pallas_call(hand_out, out_shape=result, in_specs=[anywhere] * 4, out_s...  1.9 us

profile of v10, /device:TPU:0, one launch (start us, length us, event | category | flops | bytes accessed | tf_op | source)
XLA Modules:
  0.0 63.1 jit_solution(9813748154838812248)
XLA Ops:
  0.6 60.6 %shard_map.84 = (bf16[512,256]{1,0:T(8,128)(2,1)S(1)}, bf16[512,256]{1,0:T(8,128)(2,1)S(1)}, f32[6,256,256]{2,1,0:T(8,128)S(1)}, f32[6,256,256]{2,1,0:T(8,128)S(1)}) custom-call(bf16[512,256]{1,0:T(8,128)(2,1)} %tok.1, bf16[512,256]{1,0:T(8,128)(2,1)} %cot.1, bf16[6,256,256]{2,1,0:T(8,128)(2,1)} %bitcast.4, bf16[6,256,256]{2,1,0:T(8,128)(2,1)} %bitcast.5, ...), custom_call_target="tpu_custom_call" | custom-call | tf_op jit(solution)/shard_map/pallas_call | solution.py:510
  61.2 1.9 %shard_map.85 = (bf16[512,256]{1,0:T(8,128)(2,1)}, bf16[512,256]{1,0:T(8,128)(2,1)}, f32[6,256,256]{2,1,0:T(8,128)}, f32[6,256,256]{2,1,0:T(8,128)}) custom-call(bf16[512,256]{1,0:T(8,128)(2,1)S(1)} %get-tuple-element.12.refs_0_, bf16[512,256]{1,0:T(8,128)(2,1)S(1)} %get-tuple-element.13.refs_1_, f32[6,256,256]{2,1,0:T(8,128)S(1)} %get-tuple-element.14.refs_2_, ...), custom_call_target="tpu_custom_call" | custom-call | tf_op jit(solution)/shard_map/pallas_call | solution.py:554
